TPU v7x, 512 devices: a whole 4x4x16 slice. The times are simulated.
512 devices in a mesh: frame: 16 (over z_hi, y), pix: 32 (over z_lo, x, core).
Axes of the slice: x: 4, y: 4, z: 16 (z_hi: 4, z_lo: 4; z = z_hi * 4 + z_lo), core: 2. Of those that a mesh axis runs over, the one named last changes fastest.
Arguments:
- intensity: bfloat16 [512, 262144], P('frame', 'pix'), may hold values from 0.099609375 to 10
- labels: int32 [262144], P('pix'), may hold values from -1 to 63, as said below
Outputs:
- two_time: float32 [64, 512, 512], P('pix', 'frame')
Inputs may be any that keep to these rules, and one draw needn't show every extreme that they name: `labels`: on the pixels of one index of pix every q-bin label occurs at least 64 and at most 128 times and -1 occurs; one label occurs exactly 128 times on every index of pix.
All inputs are finite; a program needn't handle non-finite values.
Results may differ from a plain program's by a relative error of at most 0.0003.
Values may be sent and summed in bfloat16 or wider, within the bound.
A program may use at most 64 MiB of HBM per device.

v0:
```python
import jax
import jax.numpy as jnp
from jax import lax
from jax.sharding import PartitionSpec as P

BINS = 64


def pack_bins(intensity, labels):
    pixels = labels.shape[0]
    bin_depth = pixels // BINS
    pix_order = jnp.argsort(labels, stable=True)
    sorted_labels = labels[pix_order]
    bin_ids = lax.iota(jnp.int32, BINS)
    starts = jnp.searchsorted(sorted_labels, bin_ids, side="left")
    bin_ends = jnp.searchsorted(sorted_labels, bin_ids, side="right")
    counts = bin_ends - starts
    offsets = lax.iota(jnp.int32, bin_depth)
    source = jnp.clip(starts[:, None] + offsets[None, :], 0, pixels - 1)
    is_valid = (offsets[None, :] < counts[:, None]).reshape(1, -1)
    picked = jnp.take(pix_order, source.reshape(-1))
    packed = jnp.take(intensity, picked, axis=1)
    packed = jnp.where(is_valid, packed, jnp.zeros_like(packed))
    return (packed, counts)


def body(intensity, labels):
    frame_rows = intensity.shape[0]
    packed, counts = pack_bins(intensity, labels)
    bin_depth = labels.shape[0] // BINS
    per_device = BINS // lax.axis_size("pix")
    frame_start = lax.axis_index("frame") * frame_rows
    gathered = lax.all_gather(packed, "frame", axis=0, tiled=True)
    all_frames = gathered.shape[0]
    other = gathered.reshape(all_frames, BINS, bin_depth)
    own_pixels = packed.reshape(frame_rows, BINS, bin_depth)
    local_totals = jnp.sum(other, axis=2, dtype=jnp.float32).T
    all_totals, all_counts = lax.psum((local_totals, counts.astype(jnp.float32)), "pix")
    gram = lax.psum_scatter(
        jnp.einsum("tbk,ubk->btu", own_pixels, other, preferred_element_type=jnp.float32),
        "pix",
        scatter_dimension=0,
        tiled=True,
    )
    bin_start = lax.axis_index("pix") * per_device
    totals = lax.dynamic_slice_in_dim(all_totals, bin_start, per_device, 0)
    bin_counts = lax.dynamic_slice_in_dim(all_counts, bin_start, per_device, 0)
    row_totals = lax.dynamic_slice_in_dim(totals, frame_start, frame_rows, 1)
    return bin_counts[:, None, None] * gram / (row_totals[:, :, None] * totals[:, None, :])


def solution(mesh):
    return jax.shard_map(
        body,
        mesh=mesh,
        in_specs=(P("frame", "pix"), P("pix")),
        out_specs=P("pix", "frame", None),
        check_vma=False,
    )
```

profile of v0, /device:TPU:1, one launch (start us, length us, event | category | flops | bytes accessed | tf_op | source)
XLA Modules:
  0.0 830.1 jit_solution(1501082467141679601)
XLA Ops:
  6.6 7.6 sort.17
  14.2 45.5 %gather_fusion.2 = s32[8192]{0:T(1024)S(1)} fusion(s32[8192]{0:T(1024)S(1)} %copy-done, s32[8192]{0:T(1024)S(1)} %fusion.16), kind=kCustom, calls=%fused_computation.2 | custom fusion | bytes 98304 | tf_op jit(solution)/shard_map/gather | solution.py:13
  59.7 11.6 %while.49 = (s32[]{:T(128)}, u32[64]{0:T(128)S(1)}, u32[64]{0:T(128)S(1)}, s32[8192]{0:T(1024)S(1)}, s32[]{:T(128)}, /*index=5*/s32[]{:T(128)}, s32[]{}) while((s32[]{:T(128)}, u32[64]{0:T(128)S(1)}, u32[64]{0:T(128)S(1)}, s32[8192]{0:T(1024)S(1)}, s32[]{:T(128)}, /*index=5*/s32[]{:T(128)}, s32[]{}) %tuple.62), condition=%wide.region_4.5_spmd.clone, body=%wide.region_3.4_spmd.clone.sunk | while | flops 1860 | bytes 7268 | solution.py:15
  59.7 0.8 gather_fusion.1
  60.6 0.8 gather_fusion.1
  61.4 0.8 gather_fusion.1
  64.7 0.8 gather_fusion.1
  65.5 0.8 gather_fusion.1
  66.3 0.8 gather_fusion.1
  69.6 0.8 gather_fusion.1
  70.5 0.8 gather_fusion.1
  71.2 11.6 %while.48 = (s32[]{:T(128)}, u32[64]{0:T(128)S(1)}, u32[64]{0:T(128)S(1)}, s32[8192]{0:T(1024)S(1)}, s32[]{:T(128)}, /*index=5*/s32[]{:T(128)}, s32[]{}) while((s32[]{:T(128)}, u32[64]{0:T(128)S(1)}, u32[64]{0:T(128)S(1)}, s32[8192]{0:T(1024)S(1)}, s32[]{:T(128)}, /*index=5*/s32[]{:T(128)}, s32[]{}) %tuple.74), condition=%wide.region_2.3_spmd.clone, body=%wide.region_1.2_spmd.clone.sunk | while | flops 1860 | bytes 7268 | solution.py:16
  71.3 0.8 gather_fusion
  72.1 0.8 gather_fusion
  75.4 0.8 gather_fusion
  76.2 0.8 gather_fusion
  77.1 0.8 gather_fusion
  83.1 45.5 %gather_fusion.3 = s32[8192]{0:T(1024)S(1)} fusion(s32[8192]{0:T(1024)S(1)} %get-tuple-element.136, s32[8192]{0:T(1024)S(1)} %broadcast_clamp_fusion.1), kind=kCustom, calls=%fused_computation.3 | custom fusion | bytes 98304 | tf_op jit(solution)/shard_map/jit(_take)/gather | solution.py:21
  128.8 1.0 copy.8
  129.9 29.2 %gather_fusion.4 = bf16[8192,32]{1,0:T(8,128)(2,1)} fusion(bf16[32,8192]{0,1:T(8,128)(2,1)S(1)} %copy.8, s32[8192]{0:T(1024)S(1)} %broadcast_clamp_fusion), kind=kCustom, calls=%fused_computation.4 | custom fusion | bytes 1081344 | tf_op jit(solution)/shard_map/jit(_take)/gather | solution.py:22
  159.1 7.7 fusion.8
  166.7 2.7 copy.10
  169.5 0.9 copy.9
  170.5 220.2 %all-gather.2.cloned.1.call-done = bf16[512,8192]{1,0:T(8,128)(2,1)} async-done(((bf16[32,8192]{1,0:T(8,128)(2,1)}), bf16[512,8192]{1,0:T(8,128)(2,1)}) %all-gather.2.cloned.1.call-update) | async-done | bytes 8388624 | tf_op jit(solution)/shard_map/all_gather | solution.py:33
  390.7 11.9 %copy.11 = bf16[512,8192]{0,1:T(8,128)(2,1)} copy(bf16[512,8192]{1,0:T(8,128)(2,1)} %all-gather.2.cloned.1.call-done) | data formatting | bytes 16777216 | tf_op jit(solution)/shard_map/all_gather | solution.py:33
  402.7 6.1 convert_reduce_fusion
  408.8 6.5 fusion.9
  415.4 67.2 %psum.14 = f32[64]{0:T(128)S(1)} all-reduce(f32[64]{0:T(128)S(1)} %get-tuple-element.189), channel_id=1, replica_groups=mesh['frame'=16,'pix'=32] {'pix'}, use_global_device_ids=true, to_apply=%region_5.6 | all-reduce | flops 64 | bytes 512 | tf_op jit(solution)/shard_map/psum | solution.py:38
  482.7 184.9 %all-reduce.2.cloned.1.call-done = f32[64,512]{1,0:T(8,128)} async-done(((f32[64,512]{1,0:T(8,128)}), f32[64,512]{1,0:T(8,128)}) %all-reduce.2.cloned.1.call-update) | async-done | bytes 131088 | tf_op jit(solution)/shard_map/psum | solution.py:38
  667.6 0.8 dynamic_slice.10
  669.2 152.8 %reduce-scatter.2.cloned.1.call-done = f32[2,32,512]{2,1,0:T(8,128)} async-done(((f32[64,32,512]{2,1,0:T(8,128)}), f32[2,32,512]{2,1,0:T(8,128)}) %reduce-scatter.2.cloned.1.call-update) | async-done | bytes 131088 | tf_op jit(solution)/shard_map/reduce_scatter | solution.py:39
  821.9 1.7 multiply_divide_fusion
  (129 shorter events, 13.9 us)
Async XLA Ops:
  6.5 7.6 copy-start
  6.5 384.2 %all-gather.2.cloned.1.call-start = ((), (), s32[]{:S(2)}) async-start(), calls=%async_computation.1 | async-start | bytes 8912896 | tf_op jit(solution)/shard_map/all_gather | solution.py:33
  83.0 45.8 %copy-start.2 = (bf16[32,8192]{1,0:T(8,128)(2,1)S(1)}, bf16[32,8192]{1,0:T(8,128)(2,1)}, u32[]{:S(2)}) copy-start(bf16[32,8192]{1,0:T(8,128)(2,1)} %param.6) | copy-start | bytes 1572868
  166.7 2.8 copy-start.1
  169.5 498.2 %all-reduce.2.cloned.1.call-start = ((), (), s32[]{:S(2)}) async-start(), calls=%async_computation.3 | async-start | bytes 262144 | tf_op jit(solution)/shard_map/psum | solution.py:38
  408.8 413.2 %reduce-scatter.2.cloned.1.call-start = ((), (), s32[]{:S(2)}) async-start(), calls=%async_computation.2 | async-start | bytes 4325376 | tf_op jit(solution)/shard_map/reduce_scatter | solution.py:39
Sparse Core Ops, SparseCore 0:
  169.6 221.0 all-gather.1
  408.9 258.7 all-reduce.1
  670.7 151.1 reduce-scatter.1
where the time goes:
time: 834 us; the launch traced here: 830 us
  waiting for transfers between devices  558 us (67%)
  local copies, waits for them, and re-layouts  160 us (19%)
  blocking collectives  67.2 us (8%)
  other arithmetic  24.3 us (3%)
  between operations  13.3 us (2%)
    all_gather x1, waiting for transfers between devices, body(): gathered = lax.all_gather(packed, 'frame', axis=0, tiled=True)  220 us
    psum x1, waiting for transfers between devices, body(): lax.psum((local_totals, counts.astype(jnp.float32)), 'pix')  185 us
    reduce_scatter x1, waiting for transfers between devices, body(): lax.psum_scatter(jnp.einsum('tbk,ubk->btu', own_pixels, other, preferred_...  153 us
    psum x1, blocking collectives, body(): lax.psum((local_totals, counts.astype(jnp.float32)), 'pix')  67.2 us
    gather x1, local copies, waits for them, and re-layouts, pack_bins(): sorted_labels = labels[pix_order]  45.5 us
    gather x1, local copies, waits for them, and re-layouts, pack_bins(): picked = jnp.take(pix_order, source.reshape(-1))  45.5 us
    gather x2, local copies, waits for them, and re-layouts, pack_bins(): packed = jnp.take(intensity, picked, axis=1)  30.1 us
  transfers between devices with their start and end apart: 3, of which 3 were waited for; matrix products, arithmetic and copies ran while one was open for 1% of the time, Pallas kernels for 0%

commit v1 on v0

v1 whole, which is shorter than its diff:
```python
import jax
import jax.numpy as jnp
from jax import lax
from jax.experimental import pallas as pl
from jax.experimental.pallas import tpu as pltpu
from jax.sharding import PartitionSpec as P

MESH = pl.DeviceIdType.MESH
BF16, F32, I32 = jnp.bfloat16, jnp.float32, jnp.int32
MSG = 296


def iota(shape, dim):
    return lax.broadcasted_iota(I32, shape, dim)


def slot_sources(lab, onehot, weighted, ranked, cum, idx):
    bins = iota((64, 128), 0)
    lane = iota((64, 128), 1).astype(F32)
    for i in range(64):
        member = (lab[i : i + 1, :] == bins).astype(F32)
        onehot[pl.ds(i * 64, 64), :] = member.astype(BF16)
        weighted[0:64, pl.ds(i * 128, 128)] = (member * (i + 1.0)).astype(BF16)
        weighted[64:128, pl.ds(i * 128, 128)] = (member * lane).astype(BF16)
    row, col = iota((128, 256), 0), iota((128, 256), 1)
    upto = ((row <= col) | (col >= 128)).astype(F32).astype(BF16)
    cum[...] = jnp.dot(onehot[...], upto, preferred_element_type=F32)
    before = jnp.zeros((64, 128), F32)
    slot = iota((128, 128), 0).astype(F32)
    for i in range(64):
        member = onehot[pl.ds(i * 64, 64), :].astype(F32)
        through = cum[pl.ds(i * 64, 64), 0:128] + before
        rank = jnp.sum(member * through, axis=0, keepdims=True) - 1.0
        before = before + cum[pl.ds(i * 64, 64), 128:256]
        ranked[:, pl.ds(i * 128, 128)] = (slot == rank).astype(F32).astype(BF16)
    found = lax.dot_general(
        weighted[...], ranked[...], (((1,), (1,)), ((), ())), preferred_element_type=F32
    )
    idx[...] = found.astype(I32)


def kernel(
    lab_hbm, x_hbm, o_ref,
    lab, xin, onehot, weighted, ranked, cum, idx, src, packed, met, part, got, half, xgot, tcol, fin, out,
    load_sem, send_sem, met_sem, core_send, core_recv, x_send, x_recv, fin_send, fin_recv,
):
    f, p = lax.axis_index("frame"), lax.axis_index("pix")
    zh, y = f // 4, f % 4
    zl, x, c = p // 8, (p // 2) % 4, p % 2
    z = zh * 4 + zl
    own_bin = zl * 16 + f
    owner_p = own_bin // 2
    to_self = jnp.logical_and(owner_p == p, f % 2 == c)

    load_lab = pltpu.make_async_copy(lab_hbm, lab, load_sem.at[0])
    load_x = pltpu.make_async_copy(x_hbm, xin, load_sem.at[1])
    load_lab.start()
    load_x.start()

    def place(j):
        n = j // 4
        dz = jnp.where(n % 2 == 1, 8 + (n + 1) // 2, 8 - n // 2)
        tz, ty = (z + dz) % 16, (y + j + 1) % 4
        tzl, tf = tz % 4, (tz // 4) * 4 + ty
        return tf, tzl * 8 + p % 8, tzl * 16 + tf

    barrier = pltpu.get_barrier_semaphore()

    def greet(tf, tp):
        pl.semaphore_signal(barrier, inc=1, device_id={"frame": tf, "pix": tp}, device_id_type=MESH)

    def greet_step(j, carry):
        tf, tp, _ = place(j)
        greet(tf, tp)
        return carry

    lax.fori_loop(0, 63, greet_step, 0)
    other_core = zl * 8 + x * 2 + (1 - c)
    greet(f, other_core)
    for d in range(1, 4):
        greet(f, zl * 8 + ((x + d) % 4) * 2 + c)
    for b in range(2):
        for xs in range(4):
            sf, sp = (2 * p + b) % 16, zl * 8 + xs * 2 + f % 2
            pl.when(jnp.logical_or(sf != f, sp != p))(lambda: greet(sf, sp))

    load_lab.wait()
    slot_sources(lab, onehot, weighted, ranked, cum, idx)
    load_x.wait()
    for i in range(64):
        a = (xin[0:16, pl.ds(i * 128, 128)].astype(F32) * 2048.0).astype(I32)
        b = (xin[16:32, pl.ds(i * 128, 128)].astype(F32) * 2048.0).astype(I32)
        src[pl.ds(i * 16, 16), :] = a + b * 65536

    pl.semaphore_wait(barrier, 75 - to_self.astype(I32))

    def pack(r, j):
        tile = jnp.broadcast_to(idx[pl.ds(r, 1), :], (8, 128))
        lane = jnp.broadcast_to(idx[pl.ds(64 + r, 1), :], (8, 128))
        upper = jnp.zeros((8, 128), I32)
        lower = jnp.zeros((8, 128), I32)
        for i in range(64):
            here = tile == i + 1
            up = jnp.take_along_axis(src[pl.ds(i * 16, 8), :], lane, axis=1, mode="promise_in_bounds")
            low = jnp.take_along_axis(src[pl.ds(i * 16 + 8, 8), :], lane, axis=1, mode="promise_in_bounds")
            upper = jnp.where(here, up, upper)
            lower = jnp.where(here, low, lower)
        pair = jnp.concatenate([upper, lower], axis=0)
        packed[j, 0:16, :] = ((pair & 0xFFFF).astype(F32) * (1 / 2048)).astype(BF16)
        packed[j, 16:32, :] = ((pair >> 16).astype(F32) * (1 / 2048)).astype(BF16)

    def send_step(j, carry):
        tf, tp, r = place(j)
        pack(r, j)
        pltpu.make_async_remote_copy(
            src_ref=packed.at[j],
            dst_ref=met.at[zl, pl.ds(pl.multiple_of(f * 32, 32), 32), :],
            send_sem=send_sem,
            recv_sem=met_sem,
            device_id={"frame": tf, "pix": tp},
            device_id_type=MESH,
        ).start()
        return carry

    lax.fori_loop(0, 63, send_step, 0)
    pack(own_bin, 63)
    pltpu.make_async_copy(
        packed.at[63], met.at[zl, pl.ds(pl.multiple_of(f * 32, 32), 32), :], met_sem
    ).start()
    pltpu.make_async_copy(met, met, met_sem).wait()

    right = jnp.concatenate([met[k] for k in range(4)], axis=1)
    valid = (right[0:16, :].astype(F32) > 0.0).astype(F32)
    valid = jnp.broadcast_to(valid[0:1, :], (16, 512))
    contract = (((1,), (1,)), ((), ()))

    def rows_of(parity):
        blocks = [pl.ds(pl.multiple_of((2 * i + parity) * 32, 32), 32) for i in range(8)]
        return jnp.concatenate(
            [jnp.concatenate([met[k, b, :] for b in blocks], axis=0) for k in range(4)], axis=1
        )

    part[0:256, :] = lax.dot_general(rows_of(1 - c), right, contract, preferred_element_type=F32)
    totals = lax.dot_general(valid.astype(BF16), right, contract, preferred_element_type=F32)[0:8]
    count = jnp.broadcast_to(jnp.sum(valid[0:8], axis=1, keepdims=True), (8, 512))
    part[256:264, :] = totals
    part[264:272, :] = count
    to_core = pltpu.make_async_remote_copy(
        src_ref=part, dst_ref=got, send_sem=core_send, recv_sem=core_recv,
        device_id={"frame": f, "pix": other_core}, device_id_type=MESH,
    )
    to_core.start()
    mine = lax.dot_general(rows_of(c), right, contract, preferred_element_type=F32)
    for b in range(4):
        half[b, 0:256, :] = mine[:, b * 128 : b * 128 + 128]
    to_core.wait()
    totals = totals + got[256:264, :]
    count = count[:, 0:128] + got[264:272, 0:128]
    for b in range(4):
        half[b, 0:256, :] = half[b, 0:256, :] + got[0:256, b * 128 : b * 128 + 128]
        for k in range(4):
            half[b, 256 + 8 * k : 264 + 8 * k, :] = totals[:, k * 128 : k * 128 + 128]
        half[b, 288:296, :] = count

    to_x = []
    for d in (2, 1, 3):
        tx = (x + d) % 4
        copy = pltpu.make_async_remote_copy(
            src_ref=half.at[tx], dst_ref=xgot.at[d - 1], send_sem=x_send.at[d - 1], recv_sem=x_recv.at[d - 1],
            device_id={"frame": f, "pix": zl * 8 + tx * 2 + c}, device_id_type=MESH,
        )
        copy.start()
        to_x.append(copy)
    for copy in to_x:
        copy.wait_recv()

    def summed(rows):
        return (half[x, rows, :] + xgot[0, rows, :]) + (xgot[1, rows, :] + xgot[2, rows, :])

    count = summed(pl.ds(288, 8))
    for b in range(4):
        inverse = 1.0 / summed(pl.ds(256 + 8 * b, 8))
        tcol[pl.ds(b * 128, 128), :] = jnp.broadcast_to(inverse[0:1, :], (128, 128)).T
    per_column = count / summed(pl.ds(pl.multiple_of(256 + 8 * x, 8), 8))
    per_column = jnp.broadcast_to(per_column[0:1, :], (32, 128))
    slot = own_bin % 2
    here = pl.ds(pl.multiple_of(x * 128, 128), 128)
    for i in range(8):
        tf = 2 * i + c
        rows = pl.ds(pl.multiple_of(tf * 32, 32), 32)
        fin[i] = summed(pl.ds(i * 32, 32)) * (per_column * tcol[rows, :])
        is_self = jnp.logical_and(tf == f, owner_p == p)

        @pl.when(is_self)
        def _():
            pltpu.make_async_copy(fin.at[i], out.at[slot, :, here], fin_recv).start()

        @pl.when(jnp.logical_not(is_self))
        def _():
            pltpu.make_async_remote_copy(
                src_ref=fin.at[i], dst_ref=out.at[slot, :, here], send_sem=fin_send, recv_sem=fin_recv,
                device_id={"frame": tf, "pix": owner_p}, device_id_type=MESH,
            ).start()

    pltpu.make_async_copy(out, out, fin_recv).wait()
    o_ref[...] = out[...]
    for copy in to_x:
        copy.wait_send()
    sent = packed.at[pl.ds(0, 63)]
    pltpu.make_async_copy(sent, sent, send_sem).wait()

    @pl.when(to_self)
    def _():
        some = fin.at[pl.ds(0, 7)]
        pltpu.make_async_copy(some, some, fin_send).wait()

    @pl.when(jnp.logical_not(to_self))
    def _():
        pltpu.make_async_copy(fin, fin, fin_send).wait()


def body(intensity, labels):
    dma = pltpu.SemaphoreType.DMA
    return pl.pallas_call(
        kernel,
        out_shape=jax.ShapeDtypeStruct((2, 32, 512), F32),
        in_specs=[pl.BlockSpec(memory_space=pl.ANY)] * 2,
        out_specs=pl.BlockSpec(memory_space=pltpu.VMEM),
        scratch_shapes=[
            pltpu.VMEM((64, 128), I32),
            pltpu.VMEM((32, 8192), BF16),
            pltpu.VMEM((4096, 128), BF16),
            pltpu.VMEM((128, 8192), BF16),
            pltpu.VMEM((128, 8192), BF16),
            pltpu.VMEM((4096, 256), F32),
            pltpu.VMEM((128, 128), I32),
            pltpu.VMEM((1024, 128), I32),
            pltpu.VMEM((64, 32, 128), BF16),
            pltpu.VMEM((4, 512, 128), BF16),
            pltpu.VMEM((272, 512), F32),
            pltpu.VMEM((272, 512), F32),
            pltpu.VMEM((4, MSG, 128), F32),
            pltpu.VMEM((3, MSG, 128), F32),
            pltpu.VMEM((512, 128), F32),
            pltpu.VMEM((8, 32, 128), F32),
            pltpu.VMEM((2, 32, 512), F32),
            dma((2,)), dma, dma, dma, dma, dma((3,)), dma((3,)), dma, dma,
        ],
        compiler_params=pltpu.CompilerParams(
            collective_id=0, has_side_effects=True, vmem_limit_bytes=32 << 20
        ),
        name="two_time",
    )(labels.reshape(64, 128), intensity)


def solution(mesh):
    return jax.shard_map(
        body,
        mesh=mesh,
        in_specs=(P("frame", "pix"), P("pix")),
        out_specs=P("pix", "frame", None),
        check_vma=False,
    )
```

time: 834 us -> 71.5 us (0.09)
  the two profiles are of different devices: /device:TPU:1 before, /device:TPU:3 now
where the time goes in v1:
time: 71.5 us; the launch traced here: 71.3 us
  Pallas kernels  68.8 us (96%)
  local copies, waits for them, and re-layouts  2.46 us (3%)
    pallas_call x1, Pallas kernels, body(): pl.pallas_call(kernel, out_shape=jax.ShapeDtypeStruct((2, 32, 512), F32),...  68.8 us
    unnamed x5, local copies, waits for them, and re-layouts  2.46 us

profile of v1, /device:TPU:3, one launch (start us, length us, event | category | flops | bytes accessed | tf_op | source)
XLA Modules:
  0.0 71.3 jit_solution(12956199072293316548)
XLA Ops:
  0.0 0.0 copy-start
  0.0 1.0 %copy-done = bf16[32,8192]{1,0:T(8,128)(2,1)S(1)} copy-done((bf16[32,8192]{1,0:T(8,128)(2,1)S(1)}, bf16[32,8192]{1,0:T(8,128)(2,1)}, u32[]{:S(2)}) %copy-start) | copy-done | bytes 524312
  1.0 0.0 copy-start.1
  1.0 0.8 %copy-done.1 = s32[8192]{0:T(1024)S(1)} copy-done((s32[8192]{0:T(1024)S(1)}, s32[8192]{0:T(1024)}, u32[]{:S(2)}) %copy-start.1) | copy-done | bytes 32792
  1.8 68.8 %two_time.1 = f32[2,32,512]{2,1,0:T(8,128)S(1)} custom-call(s32[64,128]{1,0:T(8,128)S(1)} %bitcast.1, bf16[32,8192]{1,0:T(8,128)(2,1)S(1)} %copy-done), custom_call_target="tpu_custom_call" | custom-call | tf_op jit(solution)/shard_map/two_time/pallas_call | solution.py:224
  70.6 0.7 copy.4
Async XLA Ops:
  0.0 1.0 %copy-start = (bf16[32,8192]{1,0:T(8,128)(2,1)S(1)}, bf16[32,8192]{1,0:T(8,128)(2,1)}, u32[]{:S(2)}) copy-start(bf16[32,8192]{1,0:T(8,128)(2,1)} %x_hbm.1) | copy-start | bytes 1572868
  1.0 0.8 %copy-start.1 = (s32[8192]{0:T(1024)S(1)}, s32[8192]{0:T(1024)}, u32[]{:S(2)}) copy-start(s32[8192]{0:T(1024)} %param.3) | copy-start | bytes 98308

commit v2 on v1

v2 whole, which is shorter than its diff:
```python
import jax
import jax.numpy as jnp
from jax import lax
from jax.experimental import pallas as pl
from jax.experimental.pallas import tpu as pltpu
from jax.sharding import PartitionSpec as P

MESH = pl.DeviceIdType.MESH
BF16, F32, I32 = jnp.bfloat16, jnp.float32, jnp.int32
LAG_X, LAG_Y = 4, 6


def iota(shape, dim):
    return lax.broadcasted_iota(I32, shape, dim)


def slot_sources(lab, onehot, weighted, ranked, cum, idx):
    bins = iota((64, 128), 0)
    lane = iota((64, 128), 1).astype(F32)
    for i in range(64):
        member = (lab[i : i + 1, :] == bins).astype(F32)
        onehot[pl.ds(i * 64, 64), :] = member.astype(BF16)
        weighted[0:64, pl.ds(i * 128, 128)] = (member * (i + 1.0)).astype(BF16)
        weighted[64:128, pl.ds(i * 128, 128)] = (member * lane).astype(BF16)
    row, col = iota((128, 256), 0), iota((128, 256), 1)
    upto = ((row <= col) | (col >= 128)).astype(F32).astype(BF16)
    cum[...] = jnp.dot(onehot[...], upto, preferred_element_type=F32)
    before = jnp.zeros((64, 128), F32)
    slot = iota((128, 128), 0).astype(F32)
    for i in range(64):
        member = onehot[pl.ds(i * 64, 64), :].astype(F32)
        through = cum[pl.ds(i * 64, 64), 0:128] + before
        rank = jnp.sum(member * through, axis=0, keepdims=True) - 1.0
        before = before + cum[pl.ds(i * 64, 64), 128:256]
        ranked[:, pl.ds(i * 128, 128)] = (slot == rank).astype(F32).astype(BF16)
    found = lax.dot_general(
        weighted[...], ranked[...], (((1,), (1,)), ((), ())), preferred_element_type=F32
    )
    idx[...] = found.astype(I32)


def kernel(
    lab_hbm, x_hbm, o_ref,
    lab, xin, onehot, weighted, ranked, cum, idx, src, packed, land, met, acc, got, tcol, fin, out,
    load_sem, z_send, z_recv, x_send, x_recv, y_send, y_recv, core_send, core_recv, fin_send, fin_recv,
):
    f, p = lax.axis_index("frame"), lax.axis_index("pix")
    zh, y = f // 4, f % 4
    zl, x, c = p // 8, (p // 2) % 4, p % 2
    z = zh * 4 + zl
    owner_c = zh // 2
    to_self = jnp.logical_and(zh % 2 == c, owner_c == c)

    load_lab = pltpu.make_async_copy(lab_hbm, lab, load_sem.at[0])
    load_x = pltpu.make_async_copy(x_hbm, xin, load_sem.at[1])
    load_lab.start()
    load_x.start()

    def along_z(dz):
        tz = lax.rem(z + dz, 16)
        return {"frame": lax.div(tz, 4) * 4 + y, "pix": lax.rem(tz, 4) * 8 + x * 2 + c}

    def along_x(tx):
        return {"frame": f, "pix": zl * 8 + tx * 2 + c}

    def along_y(ty):
        return {"frame": zh * 4 + ty, "pix": p}

    other_core = {"frame": f, "pix": zl * 8 + x * 2 + (1 - c)}

    barrier = pltpu.get_barrier_semaphore()

    def greet(device):
        pl.semaphore_signal(barrier, inc=1, device_id=device, device_id_type=MESH)

    for d in range(1, 16):
        greet(along_z(d))
    for d in range(1, 4):
        greet(along_x(lax.rem(x + d, 4)))
        greet(along_y(lax.rem(y + d, 4)))
    greet(other_core)
    for s in range(2):
        sender_zh, sender_c = 2 * c + s, zh % 2
        sender = {"frame": sender_zh * 4 + y, "pix": zl * 8 + x * 2 + sender_c}
        pl.when(jnp.logical_or(sender_zh != zh, sender_c != c))(lambda: greet(sender))

    load_lab.wait()
    slot_sources(lab, onehot, weighted, ranked, cum, idx)
    load_x.wait()
    for i in range(64):
        a = (xin[0:16, pl.ds(i * 128, 128)].astype(F32) * 2048.0).astype(I32)
        b = (xin[16:32, pl.ds(i * 128, 128)].astype(F32) * 2048.0).astype(I32)
        src[pl.ds(i * 16, 16), :] = a + b * 65536

    pl.semaphore_wait(barrier, 24 - to_self.astype(I32))

    def pack(r, slot, b):
        tile = jnp.broadcast_to(idx[pl.ds(r, 1), :], (8, 128))
        lane = jnp.broadcast_to(idx[pl.ds(64 + r, 1), :], (8, 128))
        upper = jnp.zeros((8, 128), I32)
        lower = jnp.zeros((8, 128), I32)
        for i in range(64):
            here = tile == i + 1
            up = jnp.take_along_axis(src[pl.ds(i * 16, 8), :], lane, axis=1, mode="promise_in_bounds")
            low = jnp.take_along_axis(src[pl.ds(i * 16 + 8, 8), :], lane, axis=1, mode="promise_in_bounds")
            upper = jnp.where(here, up, upper)
            lower = jnp.where(here, low, lower)
        pair = jnp.concatenate([upper, lower], axis=0)
        packed[slot, b, 0:16, :] = ((pair & 0xFFFF).astype(F32) * (1 / 2048)).astype(BF16)
        packed[slot, b, 16:32, :] = ((pair >> 16).astype(F32) * (1 / 2048)).astype(BF16)

    def slot_of(n):
        residue = lax.rem(4 - lax.div(n, 4), 4)
        return residue * 4 + lax.rem(6 - lax.rem(n, 4), 4)

    def depart(n):
        slot = slot_of(n)
        dz = lax.rem(slot, 4) * 4 + lax.div(slot, 4)
        tz = lax.rem(z + dz, 16)
        first = lax.rem(tz, 4) * 16 + lax.div(tz, 4)

        def one(b, carry):
            pack(first + 4 * b, slot, b)
            return carry

        lax.fori_loop(0, 4, one, 0)

        @pl.when(dz != 0)
        def _():
            pltpu.make_async_remote_copy(
                src_ref=packed.at[slot], dst_ref=land.at[slot], send_sem=z_send, recv_sem=z_recv.at[slot],
                device_id=along_z(dz), device_id_type=MESH,
            ).start()

        @pl.when(dz == 0)
        def _():
            pltpu.make_async_copy(packed.at[slot], land.at[slot], z_recv.at[slot]).start()

    def forward_x(n):
        slot = slot_of(n)
        pltpu.make_async_copy(land.at[slot], land.at[slot], z_recv.at[slot]).wait()
        for d in (2, 1, 3):
            tx = lax.rem(x + d, 4)
            pltpu.make_async_remote_copy(
                src_ref=land.at[slot, tx], dst_ref=met.at[slot, y, x], send_sem=x_send, recv_sem=x_recv.at[slot],
                device_id=along_x(tx), device_id_type=MESH,
            ).start()
        pltpu.make_async_copy(land.at[slot, x], met.at[slot, y, x], x_recv.at[slot]).start()

    def forward_y(n):
        slot = slot_of(n)
        pltpu.make_async_copy(met.at[slot, y], met.at[slot, y], x_recv.at[slot]).wait()
        for d in (2, 1, 3):
            pltpu.make_async_remote_copy(
                src_ref=met.at[slot, y], dst_ref=met.at[slot, y], send_sem=y_send, recv_sem=y_recv.at[lax.div(slot, 4)],
                device_id=along_y(lax.rem(y + d, 4)), device_id_type=MESH,
            ).start()

    def multiply(residue):
        group = met.at[pl.ds(residue * 4, 4), pl.ds(0, 3)]
        pltpu.make_async_copy(group, group, y_recv.at[residue]).wait()
        source_zl = lax.rem(zl + 4 - residue, 4)

        def slot(source_zh):
            return residue * 4 + lax.div(lax.rem(z + 16 - (source_zh * 4 + source_zl), 16), 4)

        slots = [slot(k) for k in range(4)]
        right = jnp.concatenate(
            [
                jnp.concatenate([met[s, ys, xs] for s in slots for ys in range(4)], axis=0)
                for xs in range(4)
            ],
            axis=1,
        )
        valid = (right[0:16, :].astype(F32) > 0.0).astype(F32)
        valid = jnp.broadcast_to(valid[0:1, :], (16, 512))

        def rows(source_zh):
            s = slot(source_zh)
            return jnp.concatenate([met[s, y, xs] for xs in range(4)], axis=1)

        left = jnp.concatenate(
            [rows(1 - c), rows(3 - c), valid.astype(BF16), rows(c), rows(2 + c)], axis=0
        )
        product = lax.dot_general(left, right, (((1,), (1,)), ((), ())), preferred_element_type=F32)
        if residue == 0:
            acc[...] = product
            acc[72:80, :] = valid[0:8, :]
        else:
            acc[0:72, :] = acc[0:72, :] + product[0:72, :]
            acc[72:80, :] = acc[72:80, :] + valid[0:8, :]
            acc[80:144, :] = acc[80:144, :] + product[80:144, :]

    def step(n, carry):
        pl.when(n < 16)(lambda: depart(n))
        pl.when(jnp.logical_and(n >= LAG_X, n < 16 + LAG_X))(lambda: forward_x(n - LAG_X))
        pl.when(jnp.logical_and(n >= LAG_Y, n < 16 + LAG_Y))(lambda: forward_y(n - LAG_Y))
        return carry

    done = 0
    for g in range(3):
        until = 4 * g + 5 + LAG_Y
        lax.fori_loop(done, until, step, 0)
        multiply((4 - g) % 4)
        done = until
    lax.fori_loop(done, 16 + LAG_Y, step, 0)
    multiply(1)

    acc[72:80, :] = jnp.broadcast_to(jnp.sum(acc[72:80, :], axis=1, keepdims=True), (8, 512))
    to_core = pltpu.make_async_remote_copy(
        src_ref=acc.at[pl.ds(0, 80)], dst_ref=got, send_sem=core_send, recv_sem=core_recv,
        device_id=other_core, device_id_type=MESH,
    )
    to_core.start()
    to_core.wait()
    totals = acc[64:72, :] + got[64:72, :]
    count = acc[72:80, :] + got[72:80, :]
    got[64:72, :] = 1.0 / totals
    per_column = jnp.broadcast_to((count / totals)[0:1, :], (32, 512))
    for k in range(2):
        target_zh = c + 2 * k
        inverse = got[64:72, pl.ds(pl.multiple_of(target_zh * 128, 128), 128)]
        tcol[...] = jnp.broadcast_to(inverse[0:1, :], (128, 128)).T
        per_row = tcol[pl.ds(pl.multiple_of(y * 32, 32), 32), :]
        per_row = jnp.concatenate([per_row] * 4, axis=1)
        whole = acc[80 + 32 * k : 112 + 32 * k, :] + got[32 * k : 32 * k + 32, :]
        fin[k] = whole * (per_column * per_row)
        is_self = jnp.logical_and(target_zh == zh, owner_c == c)

        @pl.when(is_self)
        def _():
            pltpu.make_async_copy(fin.at[k], out.at[zh % 2], fin_recv).start()

        @pl.when(jnp.logical_not(is_self))
        def _():
            pltpu.make_async_remote_copy(
                src_ref=fin.at[k], dst_ref=out.at[zh % 2], send_sem=fin_send, recv_sem=fin_recv,
                device_id={"frame": target_zh * 4 + y, "pix": zl * 8 + x * 2 + owner_c}, device_id_type=MESH,
            ).start()

    def wait_bytes(ref, sem):
        pltpu.make_async_copy(ref, ref, sem).wait()

    wait_bytes(packed.at[pl.ds(0, 15)], z_send)
    wait_bytes(land.at[:, pl.ds(0, 3)], x_send)
    wait_bytes(met.at[:, pl.ds(0, 3)], y_send)
    wait_bytes(out, fin_recv)
    o_ref[...] = out[...]
    pl.when(to_self)(lambda: wait_bytes(fin.at[0], fin_send))
    pl.when(jnp.logical_not(to_self))(lambda: wait_bytes(fin, fin_send))


def body(intensity, labels):
    dma = pltpu.SemaphoreType.DMA
    return pl.pallas_call(
        kernel,
        out_shape=jax.ShapeDtypeStruct((2, 32, 512), F32),
        in_specs=[pl.BlockSpec(memory_space=pl.ANY)] * 2,
        out_specs=pl.BlockSpec(memory_space=pltpu.VMEM),
        scratch_shapes=[
            pltpu.VMEM((64, 128), I32),
            pltpu.VMEM((32, 8192), BF16),
            pltpu.VMEM((4096, 128), BF16),
            pltpu.VMEM((128, 8192), BF16),
            pltpu.VMEM((128, 8192), BF16),
            pltpu.VMEM((4096, 256), F32),
            pltpu.VMEM((128, 128), I32),
            pltpu.VMEM((1024, 128), I32),
            pltpu.VMEM((16, 4, 32, 128), BF16),
            pltpu.VMEM((16, 4, 32, 128), BF16),
            pltpu.VMEM((16, 4, 4, 32, 128), BF16),
            pltpu.VMEM((144, 512), F32),
            pltpu.VMEM((80, 512), F32),
            pltpu.VMEM((128, 128), F32),
            pltpu.VMEM((2, 32, 512), F32),
            pltpu.VMEM((2, 32, 512), F32),
            dma((2,)), dma, dma((16,)), dma, dma((16,)), dma, dma((4,)), dma, dma, dma, dma,
        ],
        compiler_params=pltpu.CompilerParams(
            collective_id=0, has_side_effects=True, vmem_limit_bytes=60 << 20
        ),
        name="two_time",
    )(labels.reshape(64, 128), intensity)


def solution(mesh):
    return jax.shard_map(
        body,
        mesh=mesh,
        in_specs=(P("frame", "pix"), P("pix")),
        out_specs=P("pix", "frame", None),
        check_vma=False,
    )
```

time: 71.5 us -> 79.1 us (1.11)
  the two profiles are of different devices: /device:TPU:3 before, /device:TPU:1 now
where the time goes in v2:
time: 79.1 us; the launch traced here: 77.6 us
  Pallas kernels  76 us (96%)
  local copies, waits for them, and re-layouts  1.57 us (2%)
    pallas_call x1, Pallas kernels, body(): pl.pallas_call(kernel, out_shape=jax.ShapeDtypeStruct((2, 32, 512), F32),...  76 us

profile of v2, /device:TPU:1, one launch (start us, length us, event | category | flops | bytes accessed | tf_op | source)
XLA Modules:
  0.0 77.6 jit_solution(8004218207668638061)
XLA Ops:
  0.0 76.0 %two_time.1 = f32[2,32,512]{2,1,0:T(8,128)} custom-call(s32[64,128]{1,0:T(8,128)} %bitcast.1, bf16[32,8192]{1,0:T(8,128)(2,1)} %x_hbm.1), custom_call_target="tpu_custom_call" | custom-call | tf_op jit(solution)/shard_map/two_time/pallas_call | solution.py:255
  76.0 1.6 %copy.4 = f32[2,32,512]{2,1,0:T(8,128)} copy(f32[2,32,512]{2,1,0:T(8,128)} %two_time.1) | data formatting | bytes 262144

commit v3 on v2

v3 whole, which is shorter than its diff:
```python
import jax
import jax.numpy as jnp
from jax import lax
from jax.experimental import pallas as pl
from jax.experimental.pallas import tpu as pltpu
from jax.sharding import PartitionSpec as P

MESH = pl.DeviceIdType.MESH
BF16, F32, I32 = jnp.bfloat16, jnp.float32, jnp.int32


def iota(shape, dim):
    return lax.broadcasted_iota(I32, shape, dim)


def slot_sources(lab, onehot, weighted, ranked, cum, idx):
    bins = iota((64, 128), 0)
    lane = iota((64, 128), 1).astype(F32)
    for i in range(64):
        member = (lab[i : i + 1, :] == bins).astype(F32)
        onehot[pl.ds(i * 64, 64), :] = member.astype(BF16)
        weighted[0:64, pl.ds(i * 128, 128)] = (member * (i + 1.0)).astype(BF16)
        weighted[64:128, pl.ds(i * 128, 128)] = (member * lane).astype(BF16)
    row, col = iota((128, 256), 0), iota((128, 256), 1)
    upto = ((row <= col) | (col >= 128)).astype(F32).astype(BF16)
    cum[...] = jnp.dot(onehot[...], upto, preferred_element_type=F32)
    before = jnp.zeros((64, 128), F32)
    slot = iota((128, 128), 0).astype(F32)
    for i in range(64):
        member = onehot[pl.ds(i * 64, 64), :].astype(F32)
        through = cum[pl.ds(i * 64, 64), 0:128] + before
        rank = jnp.sum(member * through, axis=0, keepdims=True) - 1.0
        before = before + cum[pl.ds(i * 64, 64), 128:256]
        ranked[:, pl.ds(i * 128, 128)] = (slot == rank).astype(F32).astype(BF16)
    found = lax.dot_general(
        weighted[...], ranked[...], (((1,), (1,)), ((), ())), preferred_element_type=F32
    )
    idx[...] = found.astype(I32)


def kernel(
    lab_hbm, x_hbm, o_ref,
    lab, xin, onehot, weighted, ranked, cum, idx, src, packed, land, met, acc, got, half, xgot, tcol, fin, out,
    load_sem, z_send, z_recv, y_send, y_recv, core_send, core_recv, x_send, x_recv, fin_send, fin_recv,
):
    f, p = lax.axis_index("frame"), lax.axis_index("pix")
    zh, y = f // 4, f % 4
    zl, x, c = p // 8, (p // 2) % 4, p % 2
    z = zh * 4 + zl
    pair, h = y // 2, y % 2
    owner_c = zh // 2
    row_y = h + 2 * c
    to_self = jnp.logical_and(jnp.logical_and(row_y == y, owner_c == c), x % 2 == pair)

    load_lab = pltpu.make_async_copy(lab_hbm, lab, load_sem.at[0])
    load_x = pltpu.make_async_copy(x_hbm, xin, load_sem.at[1])
    load_lab.start()
    load_x.start()

    def along_z(dz):
        tz = lax.rem(z + dz, 16)
        return {"frame": lax.div(tz, 4) * 4 + y, "pix": lax.rem(tz, 4) * 8 + x * 2 + c}

    def along_x(tx):
        return {"frame": f, "pix": zl * 8 + tx * 2 + c}

    def along_y(ty):
        return {"frame": zh * 4 + ty, "pix": p}

    other_core = {"frame": f, "pix": zl * 8 + x * 2 + (1 - c)}

    barrier = pltpu.get_barrier_semaphore()

    def greet(device):
        pl.semaphore_signal(barrier, inc=1, device_id=device, device_id_type=MESH)

    for d in range(1, 16):
        greet(along_z(d))
    for d in range(1, 4):
        greet(along_y(lax.rem(y + d, 4)))
        greet(along_x(lax.rem(x + d, 4)))
    greet(other_core)
    for s in range(2):
        for sx in range(4):
            szh, sy, sc = 2 * c + s, 2 * (x % 2) + h, pair
            same = jnp.logical_and(jnp.logical_and(szh == zh, sy == y), jnp.logical_and(sx == x, sc == c))
            sender = {"frame": szh * 4 + sy, "pix": zl * 8 + sx * 2 + sc}
            pl.when(jnp.logical_not(same))(lambda: greet(sender))

    load_lab.wait()
    slot_sources(lab, onehot, weighted, ranked, cum, idx)
    load_x.wait()
    for i in range(64):
        a = (xin[0:16, pl.ds(i * 128, 128)].astype(F32) * 2048.0).astype(I32)
        b = (xin[16:32, pl.ds(i * 128, 128)].astype(F32) * 2048.0).astype(I32)
        src[pl.ds(i * 16, 16), :] = a + b * 65536

    pl.semaphore_wait(barrier, 30 - to_self.astype(I32))

    def pack(r, wave, n, b):
        tile = jnp.broadcast_to(idx[pl.ds(r, 1), :], (8, 128))
        lane = jnp.broadcast_to(idx[pl.ds(64 + r, 1), :], (8, 128))
        upper = jnp.zeros((8, 128), I32)
        lower = jnp.zeros((8, 128), I32)
        for i in range(64):
            here = tile == i + 1
            up = jnp.take_along_axis(src[pl.ds(i * 16, 8), :], lane, axis=1, mode="promise_in_bounds")
            low = jnp.take_along_axis(src[pl.ds(i * 16 + 8, 8), :], lane, axis=1, mode="promise_in_bounds")
            upper = jnp.where(here, up, upper)
            lower = jnp.where(here, low, lower)
        pair_of = jnp.concatenate([upper, lower], axis=0)
        packed[wave, n, b, 0:16, :] = ((pair_of & 0xFFFF).astype(F32) * (1 / 2048)).astype(BF16)
        packed[wave, n, b, 16:32, :] = ((pair_of >> 16).astype(F32) * (1 / 2048)).astype(BF16)

    def depart(t, carry):
        wave, n = lax.div(t, 16), lax.rem(t, 16)
        dz = lax.rem(8 + jnp.where(lax.rem(n, 2) == 1, lax.div(n + 1, 2), 16 - lax.div(n, 2)), 16)
        tz = lax.rem(z + dz, 16)
        first = lax.rem(tz, 4) * 16 + lax.div(tz, 4) + 8 * wave

        def one(b, carry):
            pack(first + 4 * b, wave, n, b)
            return carry

        lax.fori_loop(0, 2, one, 0)
        done = z_recv.at[wave, lax.div(n, 4)]

        @pl.when(n < 15)
        def _():
            pltpu.make_async_remote_copy(
                src_ref=packed.at[wave, n], dst_ref=land.at[wave, n], send_sem=z_send, recv_sem=done,
                device_id=along_z(dz), device_id_type=MESH,
            ).start()

        @pl.when(n == 15)
        def _():
            pltpu.make_async_copy(packed.at[wave, n], land.at[wave, n], done).start()

        return carry

    lax.fori_loop(0, 32, depart, 0)

    def forward(wave, k):
        steps = pl.ds(4 * k, 4)
        arrived = land.at[wave, steps]
        pltpu.make_async_copy(arrived, arrived, z_recv.at[wave, k]).wait()
        to = met.at[wave, steps, y]
        for b, ty in ((1 - pair, 2 - 2 * pair), (1 - pair, 3 - 2 * pair), (pair, 2 * pair + 1 - h)):
            pltpu.make_async_remote_copy(
                src_ref=land.at[wave, steps, b], dst_ref=to, send_sem=y_send, recv_sem=y_recv.at[wave],
                device_id=along_y(ty), device_id_type=MESH,
            ).start()
        pltpu.make_async_copy(land.at[wave, steps, pair], to, y_recv.at[wave]).start()

    def step_from(source_z):
        dz = lax.rem(z + 16 - source_z, 16)
        return jnp.where(dz == 0, 15, jnp.where(dz <= 8, 16 - 2 * dz, 2 * dz - 17))

    steps = [[step_from(4 * k + m) for k in range(4)] for m in range(4)]

    def multiply(wave):
        pltpu.make_async_copy(met.at[wave], met.at[wave], y_recv.at[wave]).wait()

        def frames(ys):
            return jnp.concatenate(
                [
                    jnp.concatenate([met[wave, steps[m][k], v] for k in range(4) for v in ys], axis=0)
                    for m in range(4)
                ],
                axis=1,
            )

        right = frames(range(4))
        valid = (right[0:16, :].astype(F32) > 0.0).astype(F32)
        valid = jnp.broadcast_to(valid[0:1, :], (16, 512))
        left = jnp.concatenate(
            [frames([h + 2 - 2 * c]), valid.astype(BF16), frames([row_y])], axis=0
        )
        acc[wave] = lax.dot_general(left, right, (((1,), (1,)), ((), ())), preferred_element_type=F32)
        acc[wave, 136:144, :] = jnp.broadcast_to(
            jnp.sum(valid[0:8], axis=1, keepdims=True), (8, 512)
        )

    def core_copy(wave):
        return pltpu.make_async_remote_copy(
            src_ref=acc.at[wave, pl.ds(0, 144)], dst_ref=got.at[wave],
            send_sem=core_send.at[wave], recv_sem=core_recv.at[wave],
            device_id=other_core, device_id_type=MESH,
        )

    def x_copy(wave, d):
        tx = lax.rem(x + d, 4)
        return pltpu.make_async_remote_copy(
            src_ref=half.at[wave, tx], dst_ref=xgot.at[wave, d - 1],
            send_sem=x_send.at[wave, d - 1], recv_sem=x_recv.at[wave, d - 1],
            device_id=along_x(tx), device_id_type=MESH,
        )

    def add_cores(wave):
        core_copy(wave).wait()
        totals = acc[wave, 128:136, :] + got[wave, 128:136, :]
        count = acc[wave, 136:144, 0:128] + got[wave, 136:144, 0:128]
        for b in range(4):
            block = pl.ds(b * 128, 128)
            half[wave, b, 0:128, :] = acc[wave, 144:272, block] + got[wave, 0:128, block]
            for k in range(4):
                half[wave, b, 128 + 8 * k : 136 + 8 * k, :] = totals[:, k * 128 : k * 128 + 128]
            half[wave, b, 160:168, :] = count

    def finish(wave):
        for d in (2, 1, 3):
            x_copy(wave, d).wait_recv()

        def summed(rows):
            return (half[wave, x, rows, :] + xgot[wave, 0, rows, :]) + (
                xgot[wave, 1, rows, :] + xgot[wave, 2, rows, :]
            )

        per_column = summed(pl.ds(160, 8)) / summed(pl.ds(pl.multiple_of(128 + 8 * x, 8), 8))
        per_column = jnp.broadcast_to(per_column[0:1, :], (32, 128))
        here = pl.ds(pl.multiple_of(x * 128, 128), 128)
        owner_x = 2 * wave + pair
        for k in range(4):
            inverse = 1.0 / summed(pl.ds(128 + 8 * k, 8))
            tcol[k] = jnp.broadcast_to(inverse[0:1, :], (128, 128)).T
            per_row = tcol[k, pl.ds(pl.multiple_of(row_y * 32, 32), 32), :]
            fin[4 * wave + k] = summed(pl.ds(32 * k, 32)) * (per_column * per_row)
            is_self = jnp.logical_and(to_self, jnp.logical_and(zh == k, owner_x == x))

            @pl.when(is_self)
            def _():
                pltpu.make_async_copy(fin.at[4 * wave + k], out.at[zh % 2, :, here], fin_recv).start()

            @pl.when(jnp.logical_not(is_self))
            def _():
                pltpu.make_async_remote_copy(
                    src_ref=fin.at[4 * wave + k], dst_ref=out.at[zh % 2, :, here],
                    send_sem=fin_send, recv_sem=fin_recv,
                    device_id={"frame": k * 4 + row_y, "pix": zl * 8 + owner_x * 2 + owner_c},
                    device_id_type=MESH,
                ).start()

    for k in range(4):
        forward(0, k)
    multiply(0)
    core_copy(0).start()
    add_cores(0)
    for d in (2, 1, 3):
        x_copy(0, d).start()
    for k in range(2):
        forward(1, k)
    finish(0)
    for k in range(2, 4):
        forward(1, k)
    multiply(1)
    core_copy(1).start()
    add_cores(1)
    for d in (2, 1, 3):
        x_copy(1, d).start()
    finish(1)

    def wait_bytes(ref, sem):
        pltpu.make_async_copy(ref, ref, sem).wait()

    wait_bytes(packed.at[:, pl.ds(0, 15)], z_send)
    wait_bytes(met.at[:, :, pl.ds(0, 3)], y_send)
    for wave in range(2):
        for d in (2, 1, 3):
            x_copy(wave, d).wait_send()
    pl.when(to_self)(lambda: wait_bytes(fin.at[pl.ds(0, 7)], fin_send))
    pl.when(jnp.logical_not(to_self))(lambda: wait_bytes(fin, fin_send))
    wait_bytes(out, fin_recv)
    o_ref[...] = out[...]


def body(intensity, labels):
    dma = pltpu.SemaphoreType.DMA
    return pl.pallas_call(
        kernel,
        out_shape=jax.ShapeDtypeStruct((2, 32, 512), F32),
        in_specs=[pl.BlockSpec(memory_space=pl.ANY)] * 2,
        out_specs=pl.BlockSpec(memory_space=pltpu.VMEM),
        scratch_shapes=[
            pltpu.VMEM((64, 128), I32),
            pltpu.VMEM((32, 8192), BF16),
            pltpu.VMEM((4096, 128), BF16),
            pltpu.VMEM((128, 8192), BF16),
            pltpu.VMEM((128, 8192), BF16),
            pltpu.VMEM((4096, 256), F32),
            pltpu.VMEM((128, 128), I32),
            pltpu.VMEM((1024, 128), I32),
            pltpu.VMEM((2, 16, 2, 32, 128), BF16),
            pltpu.VMEM((2, 16, 2, 32, 128), BF16),
            pltpu.VMEM((2, 16, 4, 32, 128), BF16),
            pltpu.VMEM((2, 272, 512), F32),
            pltpu.VMEM((2, 144, 512), F32),
            pltpu.VMEM((2, 4, 168, 128), F32),
            pltpu.VMEM((2, 3, 168, 128), F32),
            pltpu.VMEM((4, 128, 128), F32),
            pltpu.VMEM((8, 32, 128), F32),
            pltpu.VMEM((2, 32, 512), F32),
            dma((2,)), dma, dma((2, 4)), dma, dma((2,)), dma((2,)), dma((2,)), dma((2, 3)), dma((2, 3)), dma, dma,
        ],
        compiler_params=pltpu.CompilerParams(
            collective_id=0, has_side_effects=True, vmem_limit_bytes=60 << 20
        ),
        name="two_time",
    )(labels.reshape(64, 128), intensity)


def solution(mesh):
    return jax.shard_map(
        body,
        mesh=mesh,
        in_specs=(P("frame", "pix"), P("pix")),
        out_specs=P("pix", "frame", None),
        check_vma=False,
    )
```

time: 79.1 us -> 73.7 us (0.932)
  the two profiles are of different devices: /device:TPU:1 before, /device:TPU:14 now
where the time goes in v3:
time: 73.7 us; the launch traced here: 73.5 us
  Pallas kernels  72 us (98%)
  local copies, waits for them, and re-layouts  1.57 us (2%)
    pallas_call x1, Pallas kernels, body(): pl.pallas_call(kernel, out_shape=jax.ShapeDtypeStruct((2, 32, 512), F32),...  72 us
    unnamed x1, local copies, waits for them, and re-layouts  1.57 us

profile of v3, /device:TPU:14, one launch (start us, length us, event | category | flops | bytes accessed | tf_op | source)
XLA Modules:
  0.0 73.5 jit_solution(16514434299747525305)
XLA Ops:
  0.0 72.0 %two_time.1 = f32[2,32,512]{2,1,0:T(8,128)} custom-call(s32[64,128]{1,0:T(8,128)} %bitcast.1, bf16[32,8192]{1,0:T(8,128)(2,1)} %x_hbm.1), custom_call_target="tpu_custom_call" | custom-call | tf_op jit(solution)/shard_map/two_time/pallas_call | solution.py:278
  72.0 1.6 %copy.4 = f32[2,32,512]{2,1,0:T(8,128)} copy(f32[2,32,512]{2,1,0:T(8,128)} %two_time.1) | data formatting | bytes 262144

commit v4 on v1

--- a/solution.py
+++ b/solution.py
@@ -41,48 +41,43 @@
 
 def kernel(
     lab_hbm, x_hbm, o_ref,
-    lab, xin, onehot, weighted, ranked, cum, idx, src, packed, met, part, got, half, xgot, tcol, fin, out,
-    load_sem, send_sem, met_sem, core_send, core_recv, x_send, x_recv, fin_send, fin_recv,
+    lab, xin, onehot, weighted, ranked, cum, idx, src, packed, met, tot, tot_got, part, got, half, xgot, tcol, fin, out,
+    load_sem, line_sem, sheet_sem, send_sem, met_sem, core_send, core_recv, x_send, x_recv, fin_send, fin_recv,
 ):
     f, p = lax.axis_index("frame"), lax.axis_index("pix")
     zh, y = f // 4, f % 4
     zl, x, c = p // 8, (p // 2) % 4, p % 2
     z = zh * 4 + zl
-    own_bin = zl * 16 + f
-    owner_p = own_bin // 2
-    to_self = jnp.logical_and(owner_p == p, f % 2 == c)
+    own_bin = zl * 16 + y * 4 + zh
+    owner_p = zl * 8 + y * 2 + zh // 2
+    to_self = jnp.logical_and(owner_p == p, y % 2 == c)
 
     load_lab = pltpu.make_async_copy(lab_hbm, lab, load_sem.at[0])
     load_x = pltpu.make_async_copy(x_hbm, xin, load_sem.at[1])
     load_lab.start()
     load_x.start()
 
-    def place(j):
-        n = j // 4
-        dz = jnp.where(n % 2 == 1, 8 + (n + 1) // 2, 8 - n // 2)
-        tz, ty = (z + dz) % 16, (y + j + 1) % 4
-        tzl, tf = tz % 4, (tz // 4) * 4 + ty
-        return tf, tzl * 8 + p % 8, tzl * 16 + tf
+    def on_sheet(dy, dz):
+        ty, tz = lax.rem(y + dy, 4), lax.rem(z + dz, 16)
+        tzl, tzh = lax.rem(tz, 4), lax.div(tz, 4)
+        return tzh * 4 + ty, tzl * 8 + x * 2 + c, tzl * 16 + ty * 4 + tzh
+
+    def signal(sem, tf, tp):
+        pl.semaphore_signal(sem, inc=1, device_id={"frame": tf, "pix": tp}, device_id_type=MESH)
+
+    def beside(dx, dc):
+        return zl * 8 + lax.rem(x + dx, 4) * 2 + (c if dc == 0 else 1 - c)
+
+    others = [(dx, dc) for dx in range(4) for dc in range(2) if (dx, dc) != (0, 0)]
+    other_core = beside(0, 1)
 
     barrier = pltpu.get_barrier_semaphore()
-
-    def greet(tf, tp):
-        pl.semaphore_signal(barrier, inc=1, device_id={"frame": tf, "pix": tp}, device_id_type=MESH)
-
-    def greet_step(j, carry):
-        tf, tp, _ = place(j)
-        greet(tf, tp)
-        return carry
-
-    lax.fori_loop(0, 63, greet_step, 0)
-    other_core = zl * 8 + x * 2 + (1 - c)
-    greet(f, other_core)
+    for d in range(1, 16):
+        signal(barrier, *on_sheet(0, d)[:2])
     for d in range(1, 4):
-        greet(f, zl * 8 + ((x + d) % 4) * 2 + c)
-    for b in range(2):
-        for xs in range(4):
-            sf, sp = (2 * p + b) % 16, zl * 8 + xs * 2 + f % 2
-            pl.when(jnp.logical_or(sf != f, sp != p))(lambda: greet(sf, sp))
+        signal(barrier, *on_sheet(d, 0)[:2])
+    for dx, dc in others:
+        signal(barrier, f, beside(dx, dc))
 
     load_lab.wait()
     slot_sources(lab, onehot, weighted, ranked, cum, idx)
@@ -92,7 +87,9 @@
         b = (xin[16:32, pl.ds(i * 128, 128)].astype(F32) * 2048.0).astype(I32)
         src[pl.ds(i * 16, 16), :] = a + b * 65536
 
-    pl.semaphore_wait(barrier, 75 - to_self.astype(I32))
+    pl.semaphore_wait(barrier, 25)
+    for d in range(1, 4):
+        signal(line_sem, *on_sheet(d, 0)[:2])
 
     def pack(r, j):
         tile = jnp.broadcast_to(idx[pl.ds(r, 1), :], (8, 128))
@@ -110,7 +107,9 @@
         packed[j, 16:32, :] = ((pair >> 16).astype(F32) * (1 / 2048)).astype(BF16)
 
     def send_step(j, carry):
-        tf, tp, r = place(j)
+        n = lax.rem(j, 16)
+        dz = lax.rem(8 + jnp.where(lax.rem(n, 2) == 1, lax.div(n + 1, 2), 16 - lax.div(n, 2)), 16)
+        tf, tp, r = on_sheet(lax.div(j, 16), dz)
         pack(r, j)
         pltpu.make_async_remote_copy(
             src_ref=packed.at[j],
@@ -122,11 +121,15 @@
         ).start()
         return carry
 
-    lax.fori_loop(0, 63, send_step, 0)
-    pack(own_bin, 63)
+    lax.fori_loop(0, 15, send_step, 0)
+    pack(own_bin, 15)
     pltpu.make_async_copy(
-        packed.at[63], met.at[zl, pl.ds(pl.multiple_of(f * 32, 32), 32), :], met_sem
+        packed.at[15], met.at[zl, pl.ds(pl.multiple_of(f * 32, 32), 32), :], met_sem
     ).start()
+    pl.semaphore_wait(line_sem, 3)
+    for dx, dc in others:
+        signal(sheet_sem, f, beside(dx, dc))
+    lax.fori_loop(16, 64, send_step, 0)
     pltpu.make_async_copy(met, met, met_sem).wait()
 
     right = jnp.concatenate([met[k] for k in range(4)], axis=1)
@@ -140,39 +143,46 @@
             [jnp.concatenate([met[k, b, :] for b in blocks], axis=0) for k in range(4)], axis=1
         )
 
-    part[0:256, :] = lax.dot_general(rows_of(1 - c), right, contract, preferred_element_type=F32)
     totals = lax.dot_general(valid.astype(BF16), right, contract, preferred_element_type=F32)[0:8]
-    count = jnp.broadcast_to(jnp.sum(valid[0:8], axis=1, keepdims=True), (8, 512))
-    part[256:264, :] = totals
-    part[264:272, :] = count
-    to_core = pltpu.make_async_remote_copy(
-        src_ref=part, dst_ref=got, send_sem=core_send, recv_sem=core_recv,
-        device_id={"frame": f, "pix": other_core}, device_id_type=MESH,
-    )
-    to_core.start()
+    for b in range(4):
+        tot[8 * b : 8 * b + 8, :] = totals[:, b * 128 : b * 128 + 128]
+    tot[32:40, :] = jnp.broadcast_to(jnp.sum(valid[0:8], axis=1, keepdims=True), (8, 128))
+    theirs = lax.dot_general(rows_of(1 - c), right, contract, preferred_element_type=F32)
+    for b in range(4):
+        part[b] = theirs[:, b * 128 : b * 128 + 128]
+
+    def core_copy(source, target, k):
+        return pltpu.make_async_remote_copy(
+            src_ref=source, dst_ref=target, send_sem=core_send.at[k], recv_sem=core_recv.at[k],
+            device_id={"frame": f, "pix": other_core}, device_id_type=MESH,
+        )
+
+    to_core = [core_copy(tot, tot_got, 4)]
+    order = [(d, lax.rem(x + d, 4)) for d in (2, 1, 3, 0)]
+    to_core += [core_copy(part.at[b], got.at[b], d) for d, b in order]
+    for copy in to_core:
+        copy.start()
     mine = lax.dot_general(rows_of(c), right, contract, preferred_element_type=F32)
     for b in range(4):
         half[b, 0:256, :] = mine[:, b * 128 : b * 128 + 128]
-    to_core.wait()
-    totals = totals + got[256:264, :]
-    count = count[:, 0:128] + got[264:272, 0:128]
-    for b in range(4):
-        half[b, 0:256, :] = half[b, 0:256, :] + got[0:256, b * 128 : b * 128 + 128]
-        for k in range(4):
-            half[b, 256 + 8 * k : 264 + 8 * k, :] = totals[:, k * 128 : k * 128 + 128]
-        half[b, 288:296, :] = count
-
+    to_core[0].wait()
+    both = tot[...] + tot_got[...]
+    for b in range(4):
+        half[b, 256:MSG, :] = both
     to_x = []
-    for d in (2, 1, 3):
-        tx = (x + d) % 4
-        copy = pltpu.make_async_remote_copy(
-            src_ref=half.at[tx], dst_ref=xgot.at[d - 1], send_sem=x_send.at[d - 1], recv_sem=x_recv.at[d - 1],
-            device_id={"frame": f, "pix": zl * 8 + tx * 2 + c}, device_id_type=MESH,
-        )
-        copy.start()
-        to_x.append(copy)
+    for (d, b), copy in zip(order, to_core[1:]):
+        copy.wait()
+        half[b, 0:256, :] = half[b, 0:256, :] + got[b]
+        if d != 0:
+            copy = pltpu.make_async_remote_copy(
+                src_ref=half.at[b], dst_ref=xgot.at[d - 1], send_sem=x_send.at[d - 1], recv_sem=x_recv.at[d - 1],
+                device_id={"frame": f, "pix": beside(d, 0)}, device_id_type=MESH,
+            )
+            copy.start()
+            to_x.append(copy)
     for copy in to_x:
         copy.wait_recv()
+    pl.semaphore_wait(sheet_sem, 7)
 
     def summed(rows):
         return (half[x, rows, :] + xgot[0, rows, :]) + (xgot[1, rows, :] + xgot[2, rows, :])
@@ -183,7 +193,7 @@
         tcol[pl.ds(b * 128, 128), :] = jnp.broadcast_to(inverse[0:1, :], (128, 128)).T
     per_column = count / summed(pl.ds(pl.multiple_of(256 + 8 * x, 8), 8))
     per_column = jnp.broadcast_to(per_column[0:1, :], (32, 128))
-    slot = own_bin % 2
+    slot = zh % 2
     here = pl.ds(pl.multiple_of(x * 128, 128), 128)
     for i in range(8):
         tf = 2 * i + c
@@ -237,17 +247,20 @@
             pltpu.VMEM((1024, 128), I32),
             pltpu.VMEM((64, 32, 128), BF16),
             pltpu.VMEM((4, 512, 128), BF16),
-            pltpu.VMEM((272, 512), F32),
-            pltpu.VMEM((272, 512), F32),
+            pltpu.VMEM((40, 128), F32),
+            pltpu.VMEM((40, 128), F32),
+            pltpu.VMEM((4, 256, 128), F32),
+            pltpu.VMEM((4, 256, 128), F32),
             pltpu.VMEM((4, MSG, 128), F32),
             pltpu.VMEM((3, MSG, 128), F32),
             pltpu.VMEM((512, 128), F32),
             pltpu.VMEM((8, 32, 128), F32),
             pltpu.VMEM((2, 32, 512), F32),
-            dma((2,)), dma, dma, dma, dma, dma((3,)), dma((3,)), dma, dma,
+            dma((2,)), pltpu.SemaphoreType.REGULAR, pltpu.SemaphoreType.REGULAR, dma, dma,
+            dma((5,)), dma((5,)), dma((3,)), dma((3,)), dma, dma,
         ],
         compiler_params=pltpu.CompilerParams(
-            collective_id=0, has_side_effects=True, vmem_limit_bytes=32 << 20
+            collective_id=0, has_side_effects=True, vmem_limit_bytes=60 << 20
         ),
         name="two_time",
     )(labels.reshape(64, 128), intensity)

time: 71.5 us -> 67.6 us (0.945)
  the two profiles are of different devices: /device:TPU:3 before, /device:TPU:1 now
where the time goes in v4:
time: 67.6 us; the launch traced here: 66.6 us
  Pallas kernels  65 us (96%)
  local copies, waits for them, and re-layouts  1.57 us (2%)
    pallas_call x1, Pallas kernels, body(): pl.pallas_call(kernel, out_shape=jax.ShapeDtypeStruct((2, 32, 512), F32),...  65 us
    unnamed x1, local copies, waits for them, and re-layouts  1.57 us

profile of v4, /device:TPU:1, one launch (start us, length us, event | category | flops | bytes accessed | tf_op | source)
XLA Modules:
  0.0 66.6 jit_solution(4634346618317829564)
XLA Ops:
  0.0 65.0 %two_time.1 = f32[2,32,512]{2,1,0:T(8,128)} custom-call(s32[64,128]{1,0:T(8,128)} %bitcast.1, bf16[32,8192]{1,0:T(8,128)(2,1)} %x_hbm.1), custom_call_target="tpu_custom_call" | custom-call | tf_op jit(solution)/shard_map/two_time/pallas_call | solution.py:234
  65.0 1.6 %copy.4 = f32[2,32,512]{2,1,0:T(8,128)} copy(f32[2,32,512]{2,1,0:T(8,128)} %two_time.1) | data formatting | bytes 262144

commit v5 on v4

--- a/solution.py
+++ b/solution.py
@@ -7,7 +7,7 @@
 
 MESH = pl.DeviceIdType.MESH
 BF16, F32, I32 = jnp.bfloat16, jnp.float32, jnp.int32
-MSG = 296
+MSG = 168
 
 
 def iota(shape, dim):
@@ -137,19 +137,17 @@
     valid = jnp.broadcast_to(valid[0:1, :], (16, 512))
     contract = (((1,), (1,)), ((), ()))
 
-    def rows_of(parity):
-        blocks = [pl.ds(pl.multiple_of((2 * i + parity) * 32, 32), 32) for i in range(8)]
-        return jnp.concatenate(
+    def product(part_of, core):
+        blocks = [pl.ds(pl.multiple_of((4 * k + 2 * part_of + core) * 32, 32), 32) for k in range(4)]
+        left = jnp.concatenate(
             [jnp.concatenate([met[k, b, :] for b in blocks], axis=0) for k in range(4)], axis=1
         )
+        return lax.dot_general(left, right, contract, preferred_element_type=F32)
 
     totals = lax.dot_general(valid.astype(BF16), right, contract, preferred_element_type=F32)[0:8]
     for b in range(4):
         tot[8 * b : 8 * b + 8, :] = totals[:, b * 128 : b * 128 + 128]
     tot[32:40, :] = jnp.broadcast_to(jnp.sum(valid[0:8], axis=1, keepdims=True), (8, 128))
-    theirs = lax.dot_general(rows_of(1 - c), right, contract, preferred_element_type=F32)
-    for b in range(4):
-        part[b] = theirs[:, b * 128 : b * 128 + 128]
 
     def core_copy(source, target, k):
         return pltpu.make_async_remote_copy(
@@ -157,60 +155,69 @@
             device_id={"frame": f, "pix": other_core}, device_id_type=MESH,
         )
 
-    to_core = [core_copy(tot, tot_got, 4)]
     order = [(d, lax.rem(x + d, 4)) for d in (2, 1, 3, 0)]
-    to_core += [core_copy(part.at[b], got.at[b], d) for d, b in order]
-    for copy in to_core:
-        copy.start()
-    mine = lax.dot_general(rows_of(c), right, contract, preferred_element_type=F32)
-    for b in range(4):
-        half[b, 0:256, :] = mine[:, b * 128 : b * 128 + 128]
-    to_core[0].wait()
-    both = tot[...] + tot_got[...]
-    for b in range(4):
-        half[b, 256:MSG, :] = both
+    to_core = [core_copy(tot, tot_got, 8)]
+    to_core[0].start()
+    for m in range(2):
+        theirs = product(m, 1 - c)
+        for b in range(4):
+            part[m, b] = theirs[:, b * 128 : b * 128 + 128]
+        for d, b in order:
+            to_core.append(core_copy(part.at[m, b], got.at[m, b], 4 * m + d))
+            to_core[-1].start()
     to_x = []
-    for (d, b), copy in zip(order, to_core[1:]):
-        copy.wait()
-        half[b, 0:256, :] = half[b, 0:256, :] + got[b]
-        if d != 0:
-            copy = pltpu.make_async_remote_copy(
-                src_ref=half.at[b], dst_ref=xgot.at[d - 1], send_sem=x_send.at[d - 1], recv_sem=x_recv.at[d - 1],
-                device_id={"frame": f, "pix": beside(d, 0)}, device_id_type=MESH,
-            )
-            copy.start()
-            to_x.append(copy)
-    for copy in to_x:
-        copy.wait_recv()
-    pl.semaphore_wait(sheet_sem, 7)
-
-    def summed(rows):
-        return (half[x, rows, :] + xgot[0, rows, :]) + (xgot[1, rows, :] + xgot[2, rows, :])
-
-    count = summed(pl.ds(288, 8))
-    for b in range(4):
-        inverse = 1.0 / summed(pl.ds(256 + 8 * b, 8))
-        tcol[pl.ds(b * 128, 128), :] = jnp.broadcast_to(inverse[0:1, :], (128, 128)).T
-    per_column = count / summed(pl.ds(pl.multiple_of(256 + 8 * x, 8), 8))
-    per_column = jnp.broadcast_to(per_column[0:1, :], (32, 128))
-    slot = zh % 2
+    for m in range(2):
+        mine = product(m, c)
+        for b in range(4):
+            half[m, b, 0:128, :] = mine[:, b * 128 : b * 128 + 128]
+        if m == 0:
+            to_core[0].wait()
+            both = tot[...] + tot_got[...]
+            for b in range(4):
+                half[0, b, 128:MSG, :] = both
+        rows = pl.ds(0, 128 if m else MSG)
+        for (d, b), copy in zip(order, to_core[1 + 4 * m : 5 + 4 * m]):
+            copy.wait()
+            half[m, b, 0:128, :] = half[m, b, 0:128, :] + got[m, b]
+            if d != 0:
+                copy = pltpu.make_async_remote_copy(
+                    src_ref=half.at[m, b, rows], dst_ref=xgot.at[m, d - 1, rows],
+                    send_sem=x_send.at[m, d - 1], recv_sem=x_recv.at[m, d - 1],
+                    device_id={"frame": f, "pix": beside(d, 0)}, device_id_type=MESH,
+                )
+                copy.start()
+                to_x.append(copy)
+
+    def summed(m, rows):
+        return (half[m, x, rows, :] + xgot[m, 0, rows, :]) + (xgot[m, 1, rows, :] + xgot[m, 2, rows, :])
+
     here = pl.ds(pl.multiple_of(x * 128, 128), 128)
-    for i in range(8):
-        tf = 2 * i + c
-        rows = pl.ds(pl.multiple_of(tf * 32, 32), 32)
-        fin[i] = summed(pl.ds(i * 32, 32)) * (per_column * tcol[rows, :])
-        is_self = jnp.logical_and(tf == f, owner_p == p)
-
-        @pl.when(is_self)
-        def _():
-            pltpu.make_async_copy(fin.at[i], out.at[slot, :, here], fin_recv).start()
-
-        @pl.when(jnp.logical_not(is_self))
-        def _():
-            pltpu.make_async_remote_copy(
-                src_ref=fin.at[i], dst_ref=out.at[slot, :, here], send_sem=fin_send, recv_sem=fin_recv,
-                device_id={"frame": tf, "pix": owner_p}, device_id_type=MESH,
-            ).start()
+    for m in range(2):
+        for copy in to_x[3 * m : 3 * m + 3]:
+            copy.wait_recv()
+        if m == 0:
+            for k in range(4):
+                inverse = 1.0 / summed(0, pl.ds(128 + 8 * k, 8))
+                tcol[pl.ds(k * 128, 128), :] = jnp.broadcast_to(inverse[0:1, :], (128, 128)).T
+            per_column = summed(0, pl.ds(160, 8)) / summed(0, pl.ds(pl.multiple_of(128 + 8 * x, 8), 8))
+            per_column = jnp.broadcast_to(per_column[0:1, :], (32, 128))
+            pl.semaphore_wait(sheet_sem, 7)
+        for k in range(4):
+            tf = 4 * k + 2 * m + c
+            rows = pl.ds(pl.multiple_of(tf * 32, 32), 32)
+            fin[4 * m + k] = summed(m, pl.ds(k * 32, 32)) * (per_column * tcol[rows, :])
+            is_self = jnp.logical_and(tf == f, owner_p == p)
+
+            @pl.when(is_self)
+            def _():
+                pltpu.make_async_copy(fin.at[4 * m + k], out.at[zh % 2, :, here], fin_recv).start()
+
+            @pl.when(jnp.logical_not(is_self))
+            def _():
+                pltpu.make_async_remote_copy(
+                    src_ref=fin.at[4 * m + k], dst_ref=out.at[zh % 2, :, here], send_sem=fin_send, recv_sem=fin_recv,
+                    device_id={"frame": tf, "pix": owner_p}, device_id_type=MESH,
+                ).start()
 
     pltpu.make_async_copy(out, out, fin_recv).wait()
     o_ref[...] = out[...]
@@ -249,15 +256,15 @@
             pltpu.VMEM((4, 512, 128), BF16),
             pltpu.VMEM((40, 128), F32),
             pltpu.VMEM((40, 128), F32),
-            pltpu.VMEM((4, 256, 128), F32),
-            pltpu.VMEM((4, 256, 128), F32),
-            pltpu.VMEM((4, MSG, 128), F32),
-            pltpu.VMEM((3, MSG, 128), F32),
+            pltpu.VMEM((2, 4, 128, 128), F32),
+            pltpu.VMEM((2, 4, 128, 128), F32),
+            pltpu.VMEM((2, 4, MSG, 128), F32),
+            pltpu.VMEM((2, 3, MSG, 128), F32),
             pltpu.VMEM((512, 128), F32),
             pltpu.VMEM((8, 32, 128), F32),
             pltpu.VMEM((2, 32, 512), F32),
             dma((2,)), pltpu.SemaphoreType.REGULAR, pltpu.SemaphoreType.REGULAR, dma, dma,
-            dma((5,)), dma((5,)), dma((3,)), dma((3,)), dma, dma,
+            dma((9,)), dma((9,)), dma((2, 3)), dma((2, 3)), dma, dma,
         ],
         compiler_params=pltpu.CompilerParams(
             collective_id=0, has_side_effects=True, vmem_limit_bytes=60 << 20

time: 67.6 us -> 65.5 us (0.969)
  the two profiles are of different devices: /device:TPU:1 before, /device:TPU:17 now
where the time goes in v5:
time: 65.5 us; the launch traced here: 65.3 us
  Pallas kernels  63.7 us (97%)
  local copies, waits for them, and re-layouts  1.57 us (2%)
    pallas_call x1, Pallas kernels, body(): pl.pallas_call(kernel, out_shape=jax.ShapeDtypeStruct((2, 32, 512), F32),...  63.7 us
    unnamed x1, local copies, waits for them, and re-layouts  1.57 us

profile of v5, /device:TPU:17, one launch (start us, length us, event | category | flops | bytes accessed | tf_op | source)
XLA Modules:
  0.0 65.3 jit_solution(10174044316561730964)
XLA Ops:
  0.0 63.7 %two_time.1 = f32[2,32,512]{2,1,0:T(8,128)} custom-call(s32[64,128]{1,0:T(8,128)} %bitcast.1, bf16[32,8192]{1,0:T(8,128)(2,1)} %x_hbm.1), custom_call_target="tpu_custom_call" | custom-call | tf_op jit(solution)/shard_map/two_time/pallas_call | solution.py:241
  63.7 1.6 %copy.4 = f32[2,32,512]{2,1,0:T(8,128)} copy(f32[2,32,512]{2,1,0:T(8,128)} %two_time.1) | data formatting | bytes 262144

commit v6 on v5

--- a/solution.py
+++ b/solution.py
@@ -7,7 +7,17 @@
 
 MESH = pl.DeviceIdType.MESH
 BF16, F32, I32 = jnp.bfloat16, jnp.float32, jnp.int32
-MSG = 168
+I16 = jnp.int16
+LEVELS = 12944.0
+
+
+def code(value):
+    return ((jnp.sqrt(value) * LEVELS + 0.5).astype(I32) - 32768).astype(I16)
+
+
+def decode(coded):
+    root = (coded.astype(I32) + 32768).astype(F32) * (1.0 / LEVELS)
+    return root * root
 
 
 def iota(shape, dim):
@@ -41,8 +51,8 @@
 
 def kernel(
     lab_hbm, x_hbm, o_ref,
-    lab, xin, onehot, weighted, ranked, cum, idx, src, packed, met, tot, tot_got, part, got, half, xgot, tcol, fin, out,
-    load_sem, line_sem, sheet_sem, send_sem, met_sem, core_send, core_recv, x_send, x_recv, fin_send, fin_recv,
+    lab, xin, onehot, weighted, ranked, cum, idx, src, packed, met, tot, part, got, own, per_column, tcol, kept, xsent, xgot, fin, out,
+    load_sem, line_sem, sheet_sem, send_sem, met_sem, tot_send, tot_recv, core_send, core_recv, x_send, x_recv, fin_send, fin_recv,
 ):
     f, p = lax.axis_index("frame"), lax.axis_index("pix")
     zh, y = f // 4, f % 4
@@ -145,9 +155,18 @@
         return lax.dot_general(left, right, contract, preferred_element_type=F32)
 
     totals = lax.dot_general(valid.astype(BF16), right, contract, preferred_element_type=F32)[0:8]
-    for b in range(4):
-        tot[8 * b : 8 * b + 8, :] = totals[:, b * 128 : b * 128 + 128]
-    tot[32:40, :] = jnp.broadcast_to(jnp.sum(valid[0:8], axis=1, keepdims=True), (8, 128))
+    count = jnp.broadcast_to(jnp.sum(valid[0:1], axis=1, keepdims=True), (1, 128))
+    rows = [totals[0:1, b * 128 : b * 128 + 128] for b in range(4)]
+    tot[0] = jnp.concatenate(rows + [count] * 4, axis=0)
+    to_all = []
+    for k, (dx, dc) in enumerate(others):
+        to_all.append(
+            pltpu.make_async_remote_copy(
+                src_ref=tot.at[0], dst_ref=tot.at[k + 1], send_sem=tot_send, recv_sem=tot_recv,
+                device_id={"frame": f, "pix": beside(dx, dc)}, device_id_type=MESH,
+            )
+        )
+        to_all[-1].start()
 
     def core_copy(source, target, k):
         return pltpu.make_async_remote_copy(
@@ -156,8 +175,7 @@
         )
 
     order = [(d, lax.rem(x + d, 4)) for d in (2, 1, 3, 0)]
-    to_core = [core_copy(tot, tot_got, 8)]
-    to_core[0].start()
+    to_core = []
     for m in range(2):
         theirs = product(m, 1 - c)
         for b in range(4):
@@ -165,47 +183,49 @@
         for d, b in order:
             to_core.append(core_copy(part.at[m, b], got.at[m, b], 4 * m + d))
             to_core[-1].start()
-    to_x = []
     for m in range(2):
         mine = product(m, c)
         for b in range(4):
-            half[m, b, 0:128, :] = mine[:, b * 128 : b * 128 + 128]
-        if m == 0:
-            to_core[0].wait()
-            both = tot[...] + tot_got[...]
-            for b in range(4):
-                half[0, b, 128:MSG, :] = both
-        rows = pl.ds(0, 128 if m else MSG)
-        for (d, b), copy in zip(order, to_core[1 + 4 * m : 5 + 4 * m]):
+            own[m, b] = mine[:, b * 128 : b * 128 + 128]
+
+    theirs = tot.at[pl.ds(1, 7)]
+    pltpu.make_async_copy(theirs, theirs, tot_recv).wait()
+    both = tot[0]
+    for k in range(1, 8):
+        both = both + tot[k]
+    inverse = 1.0 / both
+    per_column[...] = inverse * both[4:5, :]
+    for k in range(4):
+        tcol[k] = jnp.broadcast_to(inverse[k : k + 1, :], (128, 128)).T
+
+    to_x = []
+    for m in range(2):
+        rows = pl.ds(pl.multiple_of((2 * m + c) * 32, 32), 32)
+        per_row = jnp.concatenate([tcol[k, rows, :] for k in range(4)], axis=0)
+        for (d, b), copy in zip(order, to_core[4 * m : 4 * m + 4]):
             copy.wait()
-            half[m, b, 0:128, :] = half[m, b, 0:128, :] + got[m, b]
-            if d != 0:
+            value = (own[m, b] + got[m, b]) * (per_row * per_column[pl.ds(b, 1), :])
+            if d == 0:
+                kept[m] = value
+            else:
+                xsent[m, d - 1] = code(value)
                 copy = pltpu.make_async_remote_copy(
-                    src_ref=half.at[m, b, rows], dst_ref=xgot.at[m, d - 1, rows],
+                    src_ref=xsent.at[m, d - 1], dst_ref=xgot.at[m, d - 1],
                     send_sem=x_send.at[m, d - 1], recv_sem=x_recv.at[m, d - 1],
                     device_id={"frame": f, "pix": beside(d, 0)}, device_id_type=MESH,
                 )
                 copy.start()
                 to_x.append(copy)
 
-    def summed(m, rows):
-        return (half[m, x, rows, :] + xgot[m, 0, rows, :]) + (xgot[m, 1, rows, :] + xgot[m, 2, rows, :])
-
+    pl.semaphore_wait(sheet_sem, 7)
     here = pl.ds(pl.multiple_of(x * 128, 128), 128)
     for m in range(2):
         for copy in to_x[3 * m : 3 * m + 3]:
             copy.wait_recv()
-        if m == 0:
-            for k in range(4):
-                inverse = 1.0 / summed(0, pl.ds(128 + 8 * k, 8))
-                tcol[pl.ds(k * 128, 128), :] = jnp.broadcast_to(inverse[0:1, :], (128, 128)).T
-            per_column = summed(0, pl.ds(160, 8)) / summed(0, pl.ds(pl.multiple_of(128 + 8 * x, 8), 8))
-            per_column = jnp.broadcast_to(per_column[0:1, :], (32, 128))
-            pl.semaphore_wait(sheet_sem, 7)
+        whole = (kept[m] + decode(xgot[m, 0])) + (decode(xgot[m, 1]) + decode(xgot[m, 2]))
         for k in range(4):
             tf = 4 * k + 2 * m + c
-            rows = pl.ds(pl.multiple_of(tf * 32, 32), 32)
-            fin[4 * m + k] = summed(m, pl.ds(k * 32, 32)) * (per_column * tcol[rows, :])
+            fin[4 * m + k] = code(whole[k * 32 : k * 32 + 32, :])
             is_self = jnp.logical_and(tf == f, owner_p == p)
 
             @pl.when(is_self)
@@ -220,9 +240,10 @@
                 ).start()
 
     pltpu.make_async_copy(out, out, fin_recv).wait()
-    o_ref[...] = out[...]
+    o_ref[...] = decode(out[...])
     for copy in to_x:
         copy.wait_send()
+    pltpu.make_async_copy(theirs, theirs, tot_send).wait()
     sent = packed.at[pl.ds(0, 63)]
     pltpu.make_async_copy(sent, sent, send_sem).wait()
 
@@ -254,17 +275,19 @@
             pltpu.VMEM((1024, 128), I32),
             pltpu.VMEM((64, 32, 128), BF16),
             pltpu.VMEM((4, 512, 128), BF16),
-            pltpu.VMEM((40, 128), F32),
-            pltpu.VMEM((40, 128), F32),
+            pltpu.VMEM((8, 8, 128), F32),
             pltpu.VMEM((2, 4, 128, 128), F32),
             pltpu.VMEM((2, 4, 128, 128), F32),
-            pltpu.VMEM((2, 4, MSG, 128), F32),
-            pltpu.VMEM((2, 3, MSG, 128), F32),
-            pltpu.VMEM((512, 128), F32),
-            pltpu.VMEM((8, 32, 128), F32),
-            pltpu.VMEM((2, 32, 512), F32),
-            dma((2,)), pltpu.SemaphoreType.REGULAR, pltpu.SemaphoreType.REGULAR, dma, dma,
-            dma((9,)), dma((9,)), dma((2, 3)), dma((2, 3)), dma, dma,
+            pltpu.VMEM((2, 4, 128, 128), F32),
+            pltpu.VMEM((8, 128), F32),
+            pltpu.VMEM((4, 128, 128), F32),
+            pltpu.VMEM((2, 128, 128), F32),
+            pltpu.VMEM((2, 3, 128, 128), I16),
+            pltpu.VMEM((2, 3, 128, 128), I16),
+            pltpu.VMEM((8, 32, 128), I16),
+            pltpu.VMEM((2, 32, 512), I16),
+            dma((2,)), pltpu.SemaphoreType.REGULAR, pltpu.SemaphoreType.REGULAR, dma, dma, dma, dma,
+            dma((8,)), dma((8,)), dma((2, 3)), dma((2, 3)), dma, dma,
         ],
         compiler_params=pltpu.CompilerParams(
             collective_id=0, has_side_effects=True, vmem_limit_bytes=60 << 20

time: 65.5 us -> 63.9 us (0.976)
  the two profiles are of different devices: /device:TPU:17 before, /device:TPU:1 now
where the time goes in v6:
time: 63.9 us; the launch traced here: 63.8 us
  Pallas kernels  62.2 us (97%)
  local copies, waits for them, and re-layouts  1.57 us (2%)
    pallas_call x1, Pallas kernels, body(): pl.pallas_call(kernel, out_shape=jax.ShapeDtypeStruct((2, 32, 512), F32),...  62.2 us
    unnamed x1, local copies, waits for them, and re-layouts  1.57 us

profile of v6, /device:TPU:1, one launch (start us, length us, event | category | flops | bytes accessed | tf_op | source)
XLA Modules:
  0.0 63.8 jit_solution(3482817440207814100)
XLA Ops:
  0.0 62.2 %two_time.1 = f32[2,32,512]{2,1,0:T(8,128)} custom-call(s32[64,128]{1,0:T(8,128)} %bitcast.1, bf16[32,8192]{1,0:T(8,128)(2,1)} %x_hbm.1), custom_call_target="tpu_custom_call" | custom-call | tf_op jit(solution)/shard_map/two_time/pallas_call | solution.py:262
  62.2 1.6 %copy.4 = f32[2,32,512]{2,1,0:T(8,128)} copy(f32[2,32,512]{2,1,0:T(8,128)} %two_time.1) | data formatting | bytes 262144

commit v7 on v6

--- a/solution.py
+++ b/solution.py
@@ -1,3 +1,5 @@
+import math
+
 import jax
 import jax.numpy as jnp
 from jax import lax
@@ -8,16 +10,18 @@
 MESH = pl.DeviceIdType.MESH
 BF16, F32, I32 = jnp.bfloat16, jnp.float32, jnp.int32
 I16 = jnp.int16
-LEVELS = 12944.0
-
-
-def code(value):
-    return ((jnp.sqrt(value) * LEVELS + 0.5).astype(I32) - 32768).astype(I16)
-
-
-def decode(coded):
-    root = (coded.astype(I32) + 32768).astype(F32) * (1.0 / LEVELS)
-    return root * root
+LOW_SUM, HIGH_SUM = 5.0, 102500.0
+LOW_OUT, HIGH_OUT = 0.0099, 25.7
+
+
+def code(value, low, high):
+    levels = 65534.0 / math.log2(high / low)
+    return ((jnp.log2(value) * levels + (0.5 - math.log2(low) * levels)).astype(I32) - 32768).astype(I16)
+
+
+def decode(coded, low, high):
+    step = math.log2(high / low) / 65534.0
+    return jnp.exp2((coded.astype(I32) + 32768).astype(F32) * step + math.log2(low))
 
 
 def iota(shape, dim):
@@ -51,16 +55,15 @@
 
 def kernel(
     lab_hbm, x_hbm, o_ref,
-    lab, xin, onehot, weighted, ranked, cum, idx, src, packed, met, tot, part, got, own, per_column, tcol, kept, xsent, xgot, fin, out,
+    lab, xin, onehot, weighted, ranked, cum, idx, src, packed, met, tot, part, got, own, inverse, tcol, kept, xsent, xgot, fin, out,
     load_sem, line_sem, sheet_sem, send_sem, met_sem, tot_send, tot_recv, core_send, core_recv, x_send, x_recv, fin_send, fin_recv,
 ):
     f, p = lax.axis_index("frame"), lax.axis_index("pix")
     zh, y = f // 4, f % 4
     zl, x, c = p // 8, (p // 2) % 4, p % 2
     z = zh * 4 + zl
-    own_bin = zl * 16 + y * 4 + zh
-    owner_p = zl * 8 + y * 2 + zh // 2
-    to_self = jnp.logical_and(owner_p == p, y % 2 == c)
+    own_bin = (zl + 2) % 4 * 16 + y * 4 + zh
+    owner_p = own_bin // 2
 
     load_lab = pltpu.make_async_copy(lab_hbm, lab, load_sem.at[0])
     load_x = pltpu.make_async_copy(x_hbm, xin, load_sem.at[1])
@@ -70,7 +73,7 @@
     def on_sheet(dy, dz):
         ty, tz = lax.rem(y + dy, 4), lax.rem(z + dz, 16)
         tzl, tzh = lax.rem(tz, 4), lax.div(tz, 4)
-        return tzh * 4 + ty, tzl * 8 + x * 2 + c, tzl * 16 + ty * 4 + tzh
+        return tzh * 4 + ty, tzl * 8 + x * 2 + c, lax.rem(tzl + 2, 4) * 16 + ty * 4 + tzh
 
     def signal(sem, tf, tp):
         pl.semaphore_signal(sem, inc=1, device_id={"frame": tf, "pix": tp}, device_id_type=MESH)
@@ -147,8 +150,14 @@
     valid = jnp.broadcast_to(valid[0:1, :], (16, 512))
     contract = (((1,), (1,)), ((), ()))
 
-    def product(part_of, core):
-        blocks = [pl.ds(pl.multiple_of((4 * k + 2 * part_of + core) * 32, 32), 32) for k in range(4)]
+    def frame_block(m, core, rel):
+        near = jnp.logical_or(rel == 0, rel == 3)
+        dz = jnp.where(rel < 2, 6, 2)
+        ty = lax.rem(y + jnp.where(near, 2 - m, 3 - 3 * m), 4)
+        return lax.div(lax.rem(z + jnp.where(core == 0, dz, 16 - dz), 16), 4) * 4 + ty
+
+    def product(m, core):
+        blocks = [pl.ds(pl.multiple_of(frame_block(m, core, rel) * 32, 32), 32) for rel in range(4)]
         left = jnp.concatenate(
             [jnp.concatenate([met[k, b, :] for b in blocks], axis=0) for k in range(4)], axis=1
         )
@@ -174,41 +183,27 @@
             device_id={"frame": f, "pix": other_core}, device_id_type=MESH,
         )
 
-    order = [(d, lax.rem(x + d, 4)) for d in (2, 1, 3, 0)]
+    order = [(d, lax.rem(x + d + 4 - y, 4)) for d in (2, 1, 3, 0)]
     to_core = []
     for m in range(2):
-        theirs = product(m, 1 - c)
-        for b in range(4):
-            part[m, b] = theirs[:, b * 128 : b * 128 + 128]
-        for d, b in order:
-            to_core.append(core_copy(part.at[m, b], got.at[m, b], 4 * m + d))
+        products = product(m, 1 - c)
+        for rel in range(4):
+            part[m, rel] = products[rel * 32 : rel * 32 + 32, :]
+        for d, rel in order:
+            to_core.append(core_copy(part.at[m, rel], got.at[m, rel], 4 * m + d))
             to_core[-1].start()
-    for m in range(2):
-        mine = product(m, c)
-        for b in range(4):
-            own[m, b] = mine[:, b * 128 : b * 128 + 128]
-
-    theirs = tot.at[pl.ds(1, 7)]
-    pltpu.make_async_copy(theirs, theirs, tot_recv).wait()
-    both = tot[0]
-    for k in range(1, 8):
-        both = both + tot[k]
-    inverse = 1.0 / both
-    per_column[...] = inverse * both[4:5, :]
-    for k in range(4):
-        tcol[k] = jnp.broadcast_to(inverse[k : k + 1, :], (128, 128)).T
-
     to_x = []
     for m in range(2):
-        rows = pl.ds(pl.multiple_of((2 * m + c) * 32, 32), 32)
-        per_row = jnp.concatenate([tcol[k, rows, :] for k in range(4)], axis=0)
-        for (d, b), copy in zip(order, to_core[4 * m : 4 * m + 4]):
+        products = product(m, c)
+        for rel in range(4):
+            own[m, rel] = products[rel * 32 : rel * 32 + 32, :]
+        for (d, rel), copy in zip(order, to_core[4 * m : 4 * m + 4]):
             copy.wait()
-            value = (own[m, b] + got[m, b]) * (per_row * per_column[pl.ds(b, 1), :])
+            value = own[m, rel] + got[m, rel]
             if d == 0:
                 kept[m] = value
             else:
-                xsent[m, d - 1] = code(value)
+                xsent[m, d - 1] = code(value, LOW_SUM, HIGH_SUM)
                 copy = pltpu.make_async_remote_copy(
                     src_ref=xsent.at[m, d - 1], dst_ref=xgot.at[m, d - 1],
                     send_sem=x_send.at[m, d - 1], recv_sem=x_recv.at[m, d - 1],
@@ -217,44 +212,45 @@
                 copy.start()
                 to_x.append(copy)
 
+    theirs = tot.at[pl.ds(1, 7)]
+    pltpu.make_async_copy(theirs, theirs, tot_recv).wait()
+    both = tot[0]
+    for k in range(1, 8):
+        both = both + tot[k]
+    inverse[...] = 1.0 / both
+    per_column = inverse[...] * both[4:5, :]
+    per_column = jnp.concatenate([per_column[k : k + 1, :] for k in range(4)], axis=1)
+    per_row = []
+    targets = [frame_block(m, c, order[3][1]) for m in range(2)]
+    for m, tf in enumerate(targets):
+        tcol[m] = jnp.broadcast_to(inverse[pl.ds(lax.div(tf, 4), 1), :], (128, 128)).T
+        rows = pl.ds(pl.multiple_of(lax.rem(tf, 4) * 32, 32), 32)
+        per_row.append(jnp.concatenate([tcol[m, rows, :]] * 4, axis=1))
+
     pl.semaphore_wait(sheet_sem, 7)
-    here = pl.ds(pl.multiple_of(x * 128, 128), 128)
-    for m in range(2):
+    to_owner = []
+    for m, tf in enumerate(targets):
         for copy in to_x[3 * m : 3 * m + 3]:
             copy.wait_recv()
-        whole = (kept[m] + decode(xgot[m, 0])) + (decode(xgot[m, 1]) + decode(xgot[m, 2]))
-        for k in range(4):
-            tf = 4 * k + 2 * m + c
-            fin[4 * m + k] = code(whole[k * 32 : k * 32 + 32, :])
-            is_self = jnp.logical_and(tf == f, owner_p == p)
-
-            @pl.when(is_self)
-            def _():
-                pltpu.make_async_copy(fin.at[4 * m + k], out.at[zh % 2, :, here], fin_recv).start()
-
-            @pl.when(jnp.logical_not(is_self))
-            def _():
-                pltpu.make_async_remote_copy(
-                    src_ref=fin.at[4 * m + k], dst_ref=out.at[zh % 2, :, here], send_sem=fin_send, recv_sem=fin_recv,
-                    device_id={"frame": tf, "pix": owner_p}, device_id_type=MESH,
-                ).start()
+        first, second, third = (decode(xgot[m, k], LOW_SUM, HIGH_SUM) for k in range(3))
+        whole = (kept[m] + first) + (second + third)
+        fin[m] = code(whole * (per_row[m] * per_column), LOW_OUT, HIGH_OUT)
+        copy = pltpu.make_async_remote_copy(
+            src_ref=fin.at[m], dst_ref=out.at[zh % 2], send_sem=fin_send.at[m], recv_sem=fin_recv,
+            device_id={"frame": tf, "pix": owner_p}, device_id_type=MESH,
+        )
+        copy.start()
+        to_owner.append(copy)
 
     pltpu.make_async_copy(out, out, fin_recv).wait()
-    o_ref[...] = decode(out[...])
+    o_ref[...] = decode(out[...], LOW_OUT, HIGH_OUT)
+    for copy in to_owner:
+        copy.wait_send()
     for copy in to_x:
         copy.wait_send()
     pltpu.make_async_copy(theirs, theirs, tot_send).wait()
     sent = packed.at[pl.ds(0, 63)]
     pltpu.make_async_copy(sent, sent, send_sem).wait()
-
-    @pl.when(to_self)
-    def _():
-        some = fin.at[pl.ds(0, 7)]
-        pltpu.make_async_copy(some, some, fin_send).wait()
-
-    @pl.when(jnp.logical_not(to_self))
-    def _():
-        pltpu.make_async_copy(fin, fin, fin_send).wait()
 
 
 def body(intensity, labels):
@@ -276,18 +272,18 @@
             pltpu.VMEM((64, 32, 128), BF16),
             pltpu.VMEM((4, 512, 128), BF16),
             pltpu.VMEM((8, 8, 128), F32),
-            pltpu.VMEM((2, 4, 128, 128), F32),
-            pltpu.VMEM((2, 4, 128, 128), F32),
-            pltpu.VMEM((2, 4, 128, 128), F32),
+            pltpu.VMEM((2, 4, 32, 512), F32),
+            pltpu.VMEM((2, 4, 32, 512), F32),
+            pltpu.VMEM((2, 4, 32, 512), F32),
             pltpu.VMEM((8, 128), F32),
-            pltpu.VMEM((4, 128, 128), F32),
             pltpu.VMEM((2, 128, 128), F32),
-            pltpu.VMEM((2, 3, 128, 128), I16),
-            pltpu.VMEM((2, 3, 128, 128), I16),
-            pltpu.VMEM((8, 32, 128), I16),
+            pltpu.VMEM((2, 32, 512), F32),
+            pltpu.VMEM((2, 3, 32, 512), I16),
+            pltpu.VMEM((2, 3, 32, 512), I16),
+            pltpu.VMEM((2, 32, 512), I16),
             pltpu.VMEM((2, 32, 512), I16),
             dma((2,)), pltpu.SemaphoreType.REGULAR, pltpu.SemaphoreType.REGULAR, dma, dma, dma, dma,
-            dma((8,)), dma((8,)), dma((2, 3)), dma((2, 3)), dma, dma,
+            dma((8,)), dma((8,)), dma((2, 3)), dma((2, 3)), dma((2,)), dma,
         ],
         compiler_params=pltpu.CompilerParams(
             collective_id=0, has_side_effects=True, vmem_limit_bytes=60 << 20

time: 63.9 us -> 59.7 us (0.934)
  Pallas kernels: 62.2 us -> 58 us
    pallas_call x1, Pallas kernels: 62.2 us -> 58 us  [body(): pl.pallas_call(kernel, out_shape=jax.ShapeDtypeStruct((2, 32, 512), F32),...]
where the time goes in v7:
time: 59.7 us; the launch traced here: 59.6 us
  Pallas kernels  58 us (97%)
  local copies, waits for them, and re-layouts  1.57 us (3%)
    pallas_call x1, Pallas kernels, body(): pl.pallas_call(kernel, out_shape=jax.ShapeDtypeStruct((2, 32, 512), F32),...  58 us
    unnamed x1, local copies, waits for them, and re-layouts  1.57 us

profile of v7, /device:TPU:1, one launch (start us, length us, event | category | flops | bytes accessed | tf_op | source)
XLA Modules:
  0.0 59.6 jit_solution(14463250142341618607)
XLA Ops:
  0.0 58.0 %two_time.1 = f32[2,32,512]{2,1,0:T(8,128)} custom-call(s32[64,128]{1,0:T(8,128)} %bitcast.1, bf16[32,8192]{1,0:T(8,128)(2,1)} %x_hbm.1), custom_call_target="tpu_custom_call" | custom-call | tf_op jit(solution)/shard_map/two_time/pallas_call | solution.py:258
  58.0 1.6 %copy.4 = f32[2,32,512]{2,1,0:T(8,128)} copy(f32[2,32,512]{2,1,0:T(8,128)} %two_time.1) | data formatting | bytes 262144

commit v8 on v7

--- a/solution.py
+++ b/solution.py
@@ -151,9 +151,8 @@
     contract = (((1,), (1,)), ((), ()))
 
     def frame_block(m, core, rel):
-        near = jnp.logical_or(rel == 0, rel == 3)
-        dz = jnp.where(rel < 2, 6, 2)
-        ty = lax.rem(y + jnp.where(near, 2 - m, 3 - 3 * m), 4)
+        dz = 6 - 4 * m
+        ty = lax.rem(y + 6 - rel, 4)
         return lax.div(lax.rem(z + jnp.where(core == 0, dz, 16 - dz), 16), 4) * 4 + ty
 
     def product(m, core):
@@ -163,19 +162,21 @@
         )
         return lax.dot_general(left, right, contract, preferred_element_type=F32)
 
-    totals = lax.dot_general(valid.astype(BF16), right, contract, preferred_element_type=F32)[0:8]
-    count = jnp.broadcast_to(jnp.sum(valid[0:1], axis=1, keepdims=True), (1, 128))
-    rows = [totals[0:1, b * 128 : b * 128 + 128] for b in range(4)]
-    tot[0] = jnp.concatenate(rows + [count] * 4, axis=0)
     to_all = []
-    for k, (dx, dc) in enumerate(others):
-        to_all.append(
-            pltpu.make_async_remote_copy(
-                src_ref=tot.at[0], dst_ref=tot.at[k + 1], send_sem=tot_send, recv_sem=tot_recv,
-                device_id={"frame": f, "pix": beside(dx, dc)}, device_id_type=MESH,
+
+    def send_totals():
+        totals = lax.dot_general(valid.astype(BF16), right, contract, preferred_element_type=F32)[0:8]
+        count = jnp.broadcast_to(jnp.sum(valid[0:1], axis=1, keepdims=True), (1, 128))
+        rows = [totals[0:1, b * 128 : b * 128 + 128] for b in range(4)]
+        tot[0] = jnp.concatenate(rows + [count] * 4, axis=0)
+        for k, (dx, dc) in enumerate(others):
+            to_all.append(
+                pltpu.make_async_remote_copy(
+                    src_ref=tot.at[0], dst_ref=tot.at[k + 1], send_sem=tot_send, recv_sem=tot_recv,
+                    device_id={"frame": f, "pix": beside(dx, dc)}, device_id_type=MESH,
+                )
             )
-        )
-        to_all[-1].start()
+            to_all[-1].start()
 
     def core_copy(source, target, k):
         return pltpu.make_async_remote_copy(
@@ -185,6 +186,7 @@
 
     order = [(d, lax.rem(x + d + 4 - y, 4)) for d in (2, 1, 3, 0)]
     to_core = []
+    to_x = []
     for m in range(2):
         products = product(m, 1 - c)
         for rel in range(4):
@@ -192,8 +194,8 @@
         for d, rel in order:
             to_core.append(core_copy(part.at[m, rel], got.at[m, rel], 4 * m + d))
             to_core[-1].start()
-    to_x = []
-    for m in range(2):
+        if m == 0:
+            send_totals()
         products = product(m, c)
         for rel in range(4):
             own[m, rel] = products[rel * 32 : rel * 32 + 32, :]

time: 59.7 us -> 59.3 us (level)
  no operation moved by 1% of the time
where the time goes in v8:
time: 59.3 us; the launch traced here: 59.2 us
  Pallas kernels  57.6 us (97%)
  local copies, waits for them, and re-layouts  1.57 us (3%)
    pallas_call x1, Pallas kernels, body(): pl.pallas_call(kernel, out_shape=jax.ShapeDtypeStruct((2, 32, 512), F32),...  57.6 us
    unnamed x1, local copies, waits for them, and re-layouts  1.57 us

profile of v8, /device:TPU:1, one launch (start us, length us, event | category | flops | bytes accessed | tf_op | source)
XLA Modules:
  0.0 59.2 jit_solution(695011512676024039)
XLA Ops:
  0.0 57.6 %two_time.1 = f32[2,32,512]{2,1,0:T(8,128)} custom-call(s32[64,128]{1,0:T(8,128)} %bitcast.1, bf16[32,8192]{1,0:T(8,128)(2,1)} %x_hbm.1), custom_call_target="tpu_custom_call" | custom-call | tf_op jit(solution)/shard_map/two_time/pallas_call | solution.py:260
  57.6 1.6 %copy.4 = f32[2,32,512]{2,1,0:T(8,128)} copy(f32[2,32,512]{2,1,0:T(8,128)} %two_time.1) | data formatting | bytes 262144

commit v9 on v8

--- a/solution.py
+++ b/solution.py
@@ -62,7 +62,13 @@
     zh, y = f // 4, f % 4
     zl, x, c = p // 8, (p // 2) % 4, p % 2
     z = zh * 4 + zl
-    own_bin = (zl + 2) % 4 * 16 + y * 4 + zh
+
+    def bin_at(by, bz):
+        turned = lax.rem(bz + 2, 16)
+        place = jnp.where(turned < 8, turned, 8 + lax.rem(turned + 2, 8))
+        return lax.div(place, 4) * 16 + by * 4 + lax.rem(place, 4)
+
+    own_bin = bin_at(y, z)
     owner_p = own_bin // 2
 
     load_lab = pltpu.make_async_copy(lab_hbm, lab, load_sem.at[0])
@@ -73,7 +79,7 @@
     def on_sheet(dy, dz):
         ty, tz = lax.rem(y + dy, 4), lax.rem(z + dz, 16)
         tzl, tzh = lax.rem(tz, 4), lax.div(tz, 4)
-        return tzh * 4 + ty, tzl * 8 + x * 2 + c, lax.rem(tzl + 2, 4) * 16 + ty * 4 + tzh
+        return tzh * 4 + ty, tzl * 8 + x * 2 + c, bin_at(ty, tz)
 
     def signal(sem, tf, tp):
         pl.semaphore_signal(sem, inc=1, device_id={"frame": tf, "pix": tp}, device_id_type=MESH)
@@ -120,9 +126,11 @@
         packed[j, 16:32, :] = ((pair >> 16).astype(F32) * (1 / 2048)).astype(BF16)
 
     def send_step(j, carry):
-        n = lax.rem(j, 16)
+        across = jnp.logical_and(j >= 8, j < 56)
+        n = jnp.where(across, lax.rem(j + 8, 16), jnp.where(j < 8, j, j - 48))
+        dy = jnp.where(across, jnp.where(j < 24, 2, jnp.where(j < 40, 1, 3)), 0)
         dz = lax.rem(8 + jnp.where(lax.rem(n, 2) == 1, lax.div(n + 1, 2), 16 - lax.div(n, 2)), 16)
-        tf, tp, r = on_sheet(lax.div(j, 16), dz)
+        tf, tp, r = on_sheet(dy, dz)
         pack(r, j)
         pltpu.make_async_remote_copy(
             src_ref=packed.at[j],
@@ -134,15 +142,15 @@
         ).start()
         return carry
 
-    lax.fori_loop(0, 15, send_step, 0)
-    pack(own_bin, 15)
-    pltpu.make_async_copy(
-        packed.at[15], met.at[zl, pl.ds(pl.multiple_of(f * 32, 32), 32), :], met_sem
-    ).start()
+    lax.fori_loop(0, 8, send_step, 0)
     pl.semaphore_wait(line_sem, 3)
     for dx, dc in others:
         signal(sheet_sem, f, beside(dx, dc))
-    lax.fori_loop(16, 64, send_step, 0)
+    lax.fori_loop(8, 63, send_step, 0)
+    pack(own_bin, 63)
+    pltpu.make_async_copy(
+        packed.at[63], met.at[zl, pl.ds(pl.multiple_of(f * 32, 32), 32), :], met_sem
+    ).start()
     pltpu.make_async_copy(met, met, met_sem).wait()
 
     right = jnp.concatenate([met[k] for k in range(4)], axis=1)
@@ -151,9 +159,7 @@
     contract = (((1,), (1,)), ((), ()))
 
     def frame_block(m, core, rel):
-        dz = 6 - 4 * m
-        ty = lax.rem(y + 6 - rel, 4)
-        return lax.div(lax.rem(z + jnp.where(core == 0, dz, 16 - dz), 16), 4) * 4 + ty
+        return (m + 2 * core) * 4 + lax.rem(y + 6 - rel, 4)
 
     def product(m, core):
         blocks = [pl.ds(pl.multiple_of(frame_block(m, core, rel) * 32, 32), 32) for rel in range(4)]
@@ -238,7 +244,7 @@
         whole = (kept[m] + first) + (second + third)
         fin[m] = code(whole * (per_row[m] * per_column), LOW_OUT, HIGH_OUT)
         copy = pltpu.make_async_remote_copy(
-            src_ref=fin.at[m], dst_ref=out.at[zh % 2], send_sem=fin_send.at[m], recv_sem=fin_recv,
+            src_ref=fin.at[m], dst_ref=out.at[own_bin % 2], send_sem=fin_send.at[m], recv_sem=fin_recv,
             device_id={"frame": tf, "pix": owner_p}, device_id_type=MESH,
         )
         copy.start()

time: 59.3 us -> 57.6 us (0.971)
  the two profiles are of different devices: /device:TPU:1 before, /device:TPU:71 now
where the time goes in v9:
time: 57.6 us; the launch traced here: 57.4 us
  Pallas kernels  55.8 us (97%)
  local copies, waits for them, and re-layouts  1.57 us (3%)
    pallas_call x1, Pallas kernels, body(): pl.pallas_call(kernel, out_shape=jax.ShapeDtypeStruct((2, 32, 512), F32),...  55.8 us
    unnamed x1, local copies, waits for them, and re-layouts  1.57 us

profile of v9, /device:TPU:71, one launch (start us, length us, event | category | flops | bytes accessed | tf_op | source)
XLA Modules:
  0.0 57.4 jit_solution(7032368465732964204)
XLA Ops:
  0.0 55.8 %two_time.1 = f32[2,32,512]{2,1,0:T(8,128)} custom-call(s32[64,128]{1,0:T(8,128)} %bitcast.1, bf16[32,8192]{1,0:T(8,128)(2,1)} %x_hbm.1), custom_call_target="tpu_custom_call" | custom-call | tf_op jit(solution)/shard_map/two_time/pallas_call | solution.py:266
  55.9 1.6 %copy.4 = f32[2,32,512]{2,1,0:T(8,128)} copy(f32[2,32,512]{2,1,0:T(8,128)} %two_time.1) | data formatting | bytes 262144

commit v10 on v9

--- a/solution.py
+++ b/solution.py
@@ -228,21 +228,18 @@
     inverse[...] = 1.0 / both
     per_column = inverse[...] * both[4:5, :]
     per_column = jnp.concatenate([per_column[k : k + 1, :] for k in range(4)], axis=1)
-    per_row = []
     targets = [frame_block(m, c, order[3][1]) for m in range(2)]
+    pl.semaphore_wait(sheet_sem, 7)
+    to_owner = []
     for m, tf in enumerate(targets):
         tcol[m] = jnp.broadcast_to(inverse[pl.ds(lax.div(tf, 4), 1), :], (128, 128)).T
         rows = pl.ds(pl.multiple_of(lax.rem(tf, 4) * 32, 32), 32)
-        per_row.append(jnp.concatenate([tcol[m, rows, :]] * 4, axis=1))
-
-    pl.semaphore_wait(sheet_sem, 7)
-    to_owner = []
-    for m, tf in enumerate(targets):
+        per_row = jnp.concatenate([tcol[m, rows, :]] * 4, axis=1)
         for copy in to_x[3 * m : 3 * m + 3]:
             copy.wait_recv()
         first, second, third = (decode(xgot[m, k], LOW_SUM, HIGH_SUM) for k in range(3))
         whole = (kept[m] + first) + (second + third)
-        fin[m] = code(whole * (per_row[m] * per_column), LOW_OUT, HIGH_OUT)
+        fin[m] = code(whole * (per_row * per_column), LOW_OUT, HIGH_OUT)
         copy = pltpu.make_async_remote_copy(
             src_ref=fin.at[m], dst_ref=out.at[own_bin % 2], send_sem=fin_send.at[m], recv_sem=fin_recv,
             device_id={"frame": tf, "pix": owner_p}, device_id_type=MESH,

time: 57.6 us -> 57.6 us (level)
  no operation moved by 1% of the time
where the time goes in v10:
time: 57.6 us; the launch traced here: 57.4 us
  Pallas kernels  55.8 us (97%)
  local copies, waits for them, and re-layouts  1.57 us (3%)
    pallas_call x1, Pallas kernels, body(): pl.pallas_call(kernel, out_shape=jax.ShapeDtypeStruct((2, 32, 512), F32),...  55.8 us
    unnamed x1, local copies, waits for them, and re-layouts  1.57 us

profile of v10, /device:TPU:71, one launch (start us, length us, event | category | flops | bytes accessed | tf_op | source)
XLA Modules:
  0.0 57.4 jit_solution(4973581839031835983)
XLA Ops:
  0.0 55.8 %two_time.1 = f32[2,32,512]{2,1,0:T(8,128)} custom-call(s32[64,128]{1,0:T(8,128)} %bitcast.1, bf16[32,8192]{1,0:T(8,128)(2,1)} %x_hbm.1), custom_call_target="tpu_custom_call" | custom-call | tf_op jit(solution)/shard_map/two_time/pallas_call | solution.py:263
  55.8 1.6 %copy.4 = f32[2,32,512]{2,1,0:T(8,128)} copy(f32[2,32,512]{2,1,0:T(8,128)} %two_time.1) | data formatting | bytes 262144
